TPU v7x, 128 devices: a whole 4x4x4 slice. The times are simulated.
128 devices in a mesh: row: 8 (over z_hi, x), col: 16 (over z_lo, y, core).
Axes of the slice: x: 4, y: 4, z: 4 (z_hi: 2, z_lo: 2; z = z_hi * 2 + z_lo), core: 2. Of those that a mesh axis runs over, the one named last changes fastest.
Arguments:
- nodes: bfloat16 [262144, 512], P(('row', 'col')), may hold values from -6 to 6
- send_list: int32 [128, 4, 4], P(('row', 'col')), may hold values from 0 to 15
- adj_index: int32 [128, 16, 4], P(('row', 'col')), may hold values from 0 to 31, as said below
- adj_weight: bfloat16 [2048, 4, 128, 128], P(('row', 'col')), may hold values from -0.25 to 0.25
- dec_send: int32 [128, 2, 4], P(('row', 'col')), may hold values from 0 to 15
- dec_index: int32 [128, 16, 3], P(('row', 'col')), may hold values from 0 to 23, as said below
- dec_weight: bfloat16 [2048, 3, 128, 128], P(('row', 'col')), may hold values from -0.3125 to 0.3125
- hidden_mask: int32 [128, 16], P(('row', 'col')), may hold values from 0 to 1, as said below
- target: bfloat16 [262144, 227], P(('row', 'col')), may hold values from -6 to 6
- w_msg: bfloat16 [512, 512], replicated, may hold values from -0.25 to 0.25
- w_update: bfloat16 [512, 512], replicated, may hold values from -0.25 to 0.25
- w_aggregate: bfloat16 [512, 512], replicated, may hold values from -0.25 to 0.25
- w_output: bfloat16 [512, 512], replicated, may hold values from -0.25 to 0.25
- w_decode: bfloat16 [512, 512], replicated, may hold values from -0.25 to 0.25
- w_head: bfloat16 [512, 227], replicated, may hold values from -0.25 to 0.25
Outputs:
- latent_grad: float32 [262144, 512], P(('row', 'col'))
- msg_grad: float32 [512, 512], replicated
- update_grad: float32 [512, 512], replicated
- aggregate_grad: float32 [512, 512], replicated
- output_grad: float32 [512, 512], replicated
- decode_grad: float32 [512, 512], replicated
- head_grad: float32 [512, 227], replicated
Inputs may be any that keep to these rules, and one draw needn't show every extreme that they name: `adj_index`: slot 0 of receiver tile t is t itself and slot 1 is the halo tile 16 + t mod (16). `dec_index`: slot 0 of grid block g reads the device's own tile g mod 16. `hidden_mask`: at most 12 blocks of one device are hidden, and some device has exactly 12.
All inputs are finite; a program needn't handle non-finite values.
Results may differ from a plain program's by a relative error of at most 0.02.
Values may be sent and summed in bfloat16 or wider, within the bound.
A program may use at most 192 MiB of HBM per device.

v0:
```python
import functools

import jax
import jax.numpy as jnp
from jax import lax
from jax.experimental import pallas as pl
from jax.experimental.pallas import tpu as pltpu
from jax.sharding import PartitionSpec as P

MESH = pl.DeviceIdType.MESH
F32 = jnp.float32
BF16 = jnp.bfloat16

D = 512
OUTC = 227
TILE = 128
NT = 16
NE = 32
NR = 24
K = 4
KD = 3
SLOTS = 12
DEC_EDGES = SLOTS * KD
ADJ_EDGES = NT * K
GROUP = 4
ROWS = GROUP * TILE
CORES = 2

JOBS = (
    (0, 768, ("z", "y", "x")),
    (768, 512, ("y", "x", "z")),
    (1280, 512, ("x", "z", "y")),
    (1792, 512, ("z", "x", "y")),
    (2304, 512, ("y", "z", "x")),
)
GRAD_ROWS = 2816
GRAD_F32 = 2304
HALF = D // 2
JOB_SEMS = 17


def axes_of(rows, cols):
    if (rows, cols) == (8, 16):
        return dict(zh=2, x=4, zl=2, y=4, n=4)
    return dict(zh=1, x=2, zl=2, y=2, n=2)


def dot(a, b):
    return lax.dot_general(a, b, (((1,), (0,)), ((), ())), preferred_element_type=F32)


def dot_nt(a, b):
    return lax.dot_general(a, b, (((1,), (1,)), ((), ())), preferred_element_type=F32)


def dot_tn(a, b):
    return lax.dot_general(a, b, (((0,), (0,)), ((), ())), preferred_element_type=F32)


def sigmoid(v):
    return 0.5 * jnp.tanh(0.5 * v) + 0.5


def rows_of(ref, start, count=GROUP):
    block = ref[pl.ds(start, count)]
    return block.reshape(count * TILE, block.shape[-1])


def put_rows(ref, start, value, count=GROUP):
    ref[pl.ds(start, count)] = value.reshape(count, TILE, value.shape[-1])


def sort_plan(values, blocks=None, per=1):
    count = len(values)
    depth = -(-count // 8) * 8
    down = lax.broadcasted_iota(jnp.int32, (depth, 128), 0)
    across = lax.broadcasted_iota(jnp.int32, (depth, 128), 1)
    mine = jnp.full((depth, 128), 1000, jnp.int32)
    other = jnp.full((depth, 128), 1000, jnp.int32)
    for q, value in enumerate(values):
        mine = jnp.where(down == q, value, mine)
        other = jnp.where(across == q, value, other)
    same_before = jnp.where((other == mine) & (across < down), 1, 0)
    before = jnp.where(other < mine, 1, 0) + same_before
    rank = jnp.sum(before, axis=1, keepdims=True)
    continues = jnp.minimum(jnp.sum(same_before, axis=1, keepdims=True), 1)
    hit = jnp.where((rank == across) & (down < count), 1, 0)
    order = jnp.sum(hit * down, axis=0, keepdims=True)
    follows = jnp.sum(hit * continues, axis=0, keepdims=True)
    upto = jnp.sum(jnp.where(mine <= across, 1, 0), axis=0, keepdims=True)
    present = jnp.minimum(jnp.sum(jnp.where(mine == across, 1, 0), axis=0, keepdims=True), 1)
    group = {1: down, 3: (down * 43) >> 7, 4: down >> 2}[per]
    group_row = jnp.sum(hit * group, axis=0, keepdims=True)
    named = down
    if blocks is not None:
        for q, value in enumerate(blocks):
            named = jnp.where(down == q, value, named)
    named_row = jnp.sum(hit * named, axis=0, keepdims=True)
    return order, follows, jnp.maximum(upto - 1, 0), present, group_row, named_row


def kernel(
    sizes,
    send_ref, adj_ref, dsend_ref, didx_ref, mask_ref,
    nodes_hbm, adjw_hbm, decw_hbm, target_hbm,
    wm_hbm, wu_hbm, wa_hbm, wo_hbm, wd_hbm, wh_hbm,
    part_hbm, back_hbm, grads_hbm,
    nv, halo, adjw, decw, target, wm, wu, wa, wo, wd, wh,
    pref, msl, g2f, agg, hid, usl, redge, rgin, err, pool0, pool1, mbuf, pool4, acc,
    gbuf, cs, cr, r1, s2, r2, x4,
    plan_v, plan,
    in_sems, plan_sem, out_sem, halo_s, halo_r, edge_s, edge_r, rg_s, rg_r, hg_s, hg_r, job_s, job_r, job_l,
):
    nrow, ncol, nx, ny, nzl = sizes["rows"], sizes["cols"], sizes["x"], sizes["y"], sizes["zl"]
    nzh, n = sizes["zh"], sizes["n"]
    r = lax.axis_index("row")
    c = lax.axis_index("col")
    zh, x = lax.div(r, nx), lax.rem(r, nx)
    zl = lax.div(c, ny * CORES)
    y = lax.rem(lax.div(c, CORES), ny)
    core = lax.rem(c, CORES)
    z = zh * nzl + zl
    place = {"x": x, "y": y, "z": z}

    def peer(axis, step):
        there = lax.rem(place[axis] + step, n)
        if axis == "x":
            return (zh * nx + there, c), there
        if axis == "y":
            return (r, (zl * ny + there) * CORES + core), there
        return (lax.div(there, nzl) * nx + x, (lax.rem(there, nzl) * ny + y) * CORES + core), there

    mate = (r, c + 1 - 2 * core)
    west = (r, lax.rem(c + ncol - 1, ncol))
    east = (r, lax.rem(c + 1, ncol))
    north = (r - 1, c)
    south = (r + 1, c)
    has_north = r > 0
    has_south = r < nrow - 1

    loads = [
        pltpu.make_async_copy(src, dst, in_sems.at[i])
        for i, (src, dst) in enumerate(
            (
                (nodes_hbm, nv), (wm_hbm, wm), (wu_hbm, wu), (adjw_hbm, adjw), (wa_hbm, wa), (wo_hbm, wo),
                (decw_hbm, decw), (wd_hbm, wd), (wh_hbm, wh),
                *((target_hbm.at[:, pl.ds(g * TILE, TILE)], target.at[g]) for g in range(NT)),
            )
        )
    ]
    for load in loads:
        load.start()

    barrier = pltpu.get_barrier_semaphore()

    def greet(device):
        pl.semaphore_signal(barrier, inc=1, device_id=device, device_id_type=MESH)

    greeted = 2
    greet(west)
    greet(east)
    for axis in ("x", "y", "z"):
        for step in range(1, n):
            greet(peer(axis, step)[0])
            greeted += 1

    @pl.when(has_north)
    def _():
        greet(north)

    @pl.when(has_south)
    def _():
        greet(south)

    def send(src, dst, ssem, rsem, device):
        return pltpu.make_async_remote_copy(
            src_ref=src, dst_ref=dst, send_sem=ssem, recv_sem=rsem, device_id=device, device_id_type=MESH
        )

    loads[0].wait()
    for d in range(4):
        for b in range(4):
            pool1[d * 4 + b] = nv[send_ref[0, d, b]]
    pl.semaphore_wait(barrier, greeted + jnp.where(has_north, 1, 0) + jnp.where(has_south, 1, 0))

    halo_to = (south, north, east, west)
    halo_has = (has_south, has_north, None, None)
    from_has = (has_north, has_south, None, None)

    def when(condition, body):
        if condition is None:
            body()
        else:
            pl.when(condition)(body)

    def halo_copy(d):
        part = pl.ds(d * 4, 4)
        return send(pool1.at[part], halo.at[part], halo_s.at[d], halo_r.at[d], halo_to[d])

    for d in range(4):
        when(halo_has[d], lambda d=d: halo_copy(d).start())

    def messages(xs, at):
        pre = dot(xs, wm[...])
        s = sigmoid(pre)
        put_rows(pref, NE + at, (pre * s).astype(BF16))
        put_rows(msl, at, (s * (1.0 + pre * (1.0 - s))).astype(BF16))

    loads[1].wait()
    loads[2].wait()

    @pl.loop(0, NT // GROUP)
    def _(g):
        xs = rows_of(nv, g * GROUP)
        messages(xs, g * GROUP)
        put_rows(g2f, g * GROUP, dot(xs, wu[...]))

    def write_plan(at, rows):
        for i, row in enumerate(rows):
            plan_v[at + i : at + i + 1, :] = row

    write_plan(0, sort_plan([adj_ref[0, k, t] for t in range(NT) for k in range(K)], per=K))
    write_plan(6, sort_plan([dsend_ref[0, d, s] for d in range(2) for s in range(4)])[:4])
    write_plan(10, sort_plan([1 - mask_ref[0, g] for g in range(NT)])[:1])
    first = pltpu.make_async_copy(plan_v.at[pl.ds(0, 16)], plan.at[pl.ds(0, 16)], plan_sem.at[0])
    first.start()
    first.wait()
    hidden = [plan[10, s] for s in range(SLOTS)]
    edge_list = [(hidden[s], k) for s in range(SLOTS) for k in range(KD)]
    write_plan(16, sort_plan([didx_ref[k, 0, g] for g, k in edge_list], [g * KD + k for g, k in edge_list], KD))
    second = pltpu.make_async_copy(plan_v.at[pl.ds(16, 8)], plan.at[pl.ds(16, 8)], plan_sem.at[1])
    second.start()
    second.wait()

    for d in (3, 2, 0, 1):
        when(from_has[d], lambda d=d: halo_copy(d).wait_recv())
        if from_has[d] is not None:

            @pl.when(jnp.logical_not(from_has[d]))
            def _(d=d):
                halo[pl.ds(d * 4, 4)] = jnp.zeros((4, TILE, D), BF16)

        messages(rows_of(halo, d * 4), NT + d * 4)

    for i in (3, 4, 5):
        loads[i].wait()

    @pl.loop(0, NT // GROUP)
    def _(g):
        for i in range(GROUP):
            t = g * GROUP + i
            weights = jnp.concatenate([adjw[t * K + k] for k in range(K)], axis=1)
            picked = jnp.concatenate(
                [pref[NE + t], pref[NE + NT + t], pref[NE + adj_ref[0, 2, t]], pref[NE + adj_ref[0, 3, t]]], axis=0
            )
            agg[t] = dot(weights, picked).astype(BF16)
        upre = rows_of(g2f, g * GROUP) + dot(rows_of(agg, g * GROUP), wa[...])
        s = sigmoid(upre)
        hidden_rows = (upre * s).astype(BF16)
        put_rows(hid, g * GROUP, hidden_rows)
        put_rows(usl, g * GROUP, (s * (1.0 + upre * (1.0 - s))).astype(BF16))
        v2 = rows_of(nv, g * GROUP).astype(F32) + dot(hidden_rows, wo[...])
        put_rows(pref, g * GROUP, v2.astype(BF16))

    for d in range(4):
        when(halo_has[d], lambda d=d: halo_copy(d).wait_send())
    for d in range(2):
        for s in range(4):
            pref[NE + d * 4 + s] = pref[dsend_ref[0, d, s]]
    edges = [
        send(pref.at[pl.ds(NE, 4)], redge.at[pl.ds(4, 4)], edge_s.at[0], edge_r.at[0], west),
        send(pref.at[pl.ds(NE + 4, 4)], redge.at[pl.ds(0, 4)], edge_s.at[1], edge_r.at[1], east),
    ]
    for edge in edges:
        edge.start()
    for load in loads[6:]:
        load.wait()
    for edge in edges:
        edge.wait()
    for e in range(8):
        pref[NT + e] = redge[e]

    @pl.loop(0, SLOTS // GROUP)
    def _(g):
        goals, marks = [], []
        for i in range(GROUP):
            s = g * GROUP + i
            block = plan[10, s]
            weights = jnp.concatenate([decw[block * KD + k] for k in range(KD)], axis=1)
            picked = jnp.concatenate([pref[didx_ref[k, 0, block]] for k in range(KD)], axis=0)
            pool0[s] = dot(weights, picked).astype(BF16)
            goals.append(target[block].astype(F32))
            marks.append(jnp.full((1, TILE), mask_ref[0, block].astype(F32), F32))
        dpre = dot(rows_of(pool0, g * GROUP), wd[...])
        s = sigmoid(dpre)
        q = (dpre * s).astype(BF16)
        put_rows(pool1, g * GROUP, q)
        slope = s * (1.0 + dpre * (1.0 - s))
        residual = dot_nt(wh[...], q) - jnp.concatenate(goals, axis=1)
        residual = (jnp.concatenate(marks, axis=1) * residual).astype(BF16)
        err[:, pl.ds(pl.multiple_of(g * ROWS, ROWS), ROWS)] = residual
        dslope = (dot_tn(residual, wh[...]) * slope).astype(BF16)
        put_rows(mbuf, g * GROUP, dslope)
        put_rows(pool4, g * GROUP, dot_nt(dslope, wd[...]).astype(BF16))

    def spread(at, edges, weight, source):
        acc[...] = jnp.zeros((TILE, D), F32)

        @pl.loop(0, edges // GROUP)
        def _(h):
            total = acc[...]
            for i in range(GROUP):
                p = h * GROUP + i
                total = dot_tn(weight[plan[at + 5, p]], source[plan[at + 4, p]]) + plan[at + 1, p].astype(F32) * total
                pref[p] = total.astype(BF16)
            acc[...] = total

    def spread_of(at, tile):
        return plan[at + 3, tile].astype(F32) * pref[plan[at + 2, tile]].astype(F32)

    spread(16, DEC_EDGES, decw, pool4)
    for e in range(8):
        pref[48 + e] = spread_of(16, NT + e).astype(BF16)
    returns = [
        send(pref.at[pl.ds(48, 4)], rgin.at[pl.ds(4, 4)], rg_s.at[0], rg_r.at[0], west),
        send(pref.at[pl.ds(52, 4)], rgin.at[pl.ds(0, 4)], rg_s.at[1], rg_r.at[1], east),
    ]
    for item in returns:
        item.start()

    def job_copy(j, sem, src, dst, device):
        return send(src, dst, job_s.at[j, sem], job_r.at[j, sem], device)

    def c_copy(j):
        at, rows, _ = JOBS[j]
        return job_copy(j, 0, cs.at[pl.ds(at, rows)], cr.at[pl.ds(at, rows)], mate)

    def first_copies(j):
        at, rows, order = JOBS[j]
        quarter = rows // n
        out = []
        for step in range(1, n):
            device, there = peer(order[0], step)
            src = cs.at[pl.ds(pl.multiple_of(at + there * quarter, 16), quarter)]
            out.append(job_copy(j, step, src, r1.at[step - 1, pl.ds(at // n, quarter)], device))
        return out

    def second_copies(j):
        at, rows, order = JOBS[j]
        small = rows // (n * n)
        out = []
        for step in range(1, n):
            device, there = peer(order[1], step)
            src = s2.at[pl.ds(pl.multiple_of(at // n + there * small, 16), small)]
            out.append(job_copy(j, 3 + step, src, r2.at[step - 1, pl.ds(at // (n * n), small)], device))
        return out

    def third_copies(j):
        at, rows, order = JOBS[j]
        small = rows // (n * n)
        out = []
        for step in range(1, n):
            device, _ = peer(order[2], step)
            mine = x4.at[place[order[2]], pl.ds(at // (n * n), small)]
            out.append(job_copy(j, 6 + step, mine, mine, device))
        return out

    def small_at(j):
        at, rows, order = JOBS[j]
        quarter, small = rows // n, rows // (n * n)
        return pl.multiple_of(at + place[order[0]] * quarter + place[order[1]] * small, 16)

    def back_small(j):
        at, rows, order = JOBS[j]
        part = cr.at[pl.ds(small_at(j), rows // (n * n))]
        return [
            job_copy(j, 9 + step, part, part, peer(order[1], step)[0]) for step in range(1, n)
        ]

    def back_quarter(j):
        at, rows, order = JOBS[j]
        quarter = rows // n
        part = cr.at[pl.ds(pl.multiple_of(at + place[order[0]] * quarter, 16), quarter)]
        return [
            job_copy(j, 12 + step, part, part, peer(order[0], step)[0]) for step in range(1, n)
        ]

    def back_core(j):
        at, rows, _ = JOBS[j]
        part = pl.ds(at, rows)
        return (
            job_copy(j, 16, cr.at[part], grads_hbm.at[core, part], mate),
            pltpu.make_async_copy(cr.at[part], grads_hbm.at[core, part], job_l.at[j]),
        )

    def job_stage(j, stage_number):
        at, rows, order = JOBS[j]
        quarter, small = rows // n, rows // (n * n)
        whole = pl.ds(at, rows)
        own = pl.ds(at % GRAD_F32, rows)
        if stage_number == 0:
            low, high = gbuf[own, :HALF], gbuf[own, HALF:]
            cs[whole] = jnp.where(core == 0, high, low).astype(BF16)
            c_copy(j).start()
        elif stage_number == 1:
            c_copy(j).wait()
            low, high = gbuf[own, :HALF], gbuf[own, HALF:]
            cs[whole] = (jnp.where(core == 0, low, high) + cr[whole].astype(F32)).astype(BF16)
            for item in first_copies(j):
                item.start()
        elif stage_number == 2:
            mine = pl.ds(pl.multiple_of(at + place[order[0]] * quarter, 16), quarter)
            for item in first_copies(j):
                item.wait()
            total = cs[mine].astype(F32)
            for step in range(n - 1):
                total = total + r1[step, pl.ds(at // n, quarter)].astype(F32)
            s2[pl.ds(at // n, quarter)] = total.astype(BF16)
            for item in second_copies(j):
                item.start()
        elif stage_number == 3:
            mine = pl.ds(pl.multiple_of(at // n + place[order[1]] * small, 16), small)
            for item in second_copies(j):
                item.wait()
            total = s2[mine].astype(F32)
            for step in range(n - 1):
                total = total + r2[step, pl.ds(at // (n * n), small)].astype(F32)
            x4[place[order[2]], pl.ds(at // (n * n), small)] = total.astype(BF16)
            for item in third_copies(j):
                item.start()
        elif stage_number == 4:
            for item in third_copies(j):
                item.wait()
            total = x4[0, pl.ds(at // (n * n), small)].astype(F32)
            for other in range(1, n):
                total = total + x4[other, pl.ds(at // (n * n), small)].astype(F32)
            cr[pl.ds(small_at(j), small)] = (total * (1.0 / (nrow * ncol))).astype(BF16)
            for item in back_small(j):
                item.start()
        elif stage_number == 5:
            for item in back_small(j):
                item.wait()
            for item in back_quarter(j):
                item.start()
        elif stage_number == 6:
            for item in back_quarter(j):
                item.wait()
            for item in back_core(j):
                item.start()
        else:
            for item in back_core(j):
                item.wait()

    def gradient(at, left, right):
        for n in range(2):
            lanes = slice(n * HALF, (n + 1) * HALF)
            total = None
            for (lref, lat, count), (rref, rat) in zip(left, right):
                lhs = lref[pl.ds(lat, count)].reshape(count * TILE, D)
                rhs = rref[pl.ds(rat, count), :, lanes].reshape(count * TILE, HALF)
                term = dot_tn(lhs, rhs)
                total = term if total is None else total + term
            gbuf[pl.ds(at % GRAD_F32, D), lanes] = total

    gradient(0, [(pool0, 0, SLOTS)], [(mbuf, 0)])
    q_rows = pool1[pl.ds(0, SLOTS)].reshape(SLOTS * TILE, D)
    gbuf[512:768, :] = jnp.zeros((256, D), F32)
    gbuf[512 : 512 + OUTC, :] = dot(err[...], q_rows)
    job_stage(0, 0)

    for item in returns:
        item.wait()
    total = None
    for p in range(8):
        arrived = rgin[plan[6, p]].astype(F32)
        total = arrived if total is None else arrived + plan[7, p].astype(F32) * total
        pref[40 + p] = total.astype(BF16)

    @pl.loop(0, NT)
    def _(t):
        value = spread_of(16, t).astype(BF16).astype(F32)
        value = value + plan[9, t].astype(F32) * pref[40 + plan[8, t]].astype(F32)
        g2f[t] = value
        pool4[t] = value.astype(BF16)

    job_stage(0, 1)

    @pl.loop(0, NT // GROUP)
    def _(g):
        back = dot_nt(rows_of(pool4, g * GROUP), wo[...]) * rows_of(usl, g * GROUP).astype(F32)
        slope = back.astype(BF16)
        put_rows(pool0, g * GROUP, slope)
        put_rows(g2f, g * GROUP, rows_of(g2f, g * GROUP) + dot_nt(slope, wu[...]))
        put_rows(pool1, g * GROUP, dot_nt(slope, wa[...]).astype(BF16))

    job_stage(0, 2)
    spread(0, ADJ_EDGES, adjw, pool1)
    job_stage(0, 3)

    def message_slope(e):
        mbuf[e] = (spread_of(0, e) * msl[e].astype(F32)).astype(BF16)

    back_to = (north, south, west, east)
    back_has = (has_north, has_south, None, None)
    back_from = (has_south, has_north, None, None)

    def back_copy(d):
        part = pl.ds(d * 4, 4)
        return send(pool1.at[part], back_hbm.at[part], hg_s.at[d], hg_r.at[d], back_to[d])

    for d in range(4):

        @pl.loop(0, 4)
        def _(b, d=d):
            message_slope(NT + d * 4 + b)

        put_rows(pool1, d * 4, dot_nt(rows_of(mbuf, NT + d * 4), wm[...]).astype(BF16))
        when(back_has[d], lambda d=d: back_copy(d).start())

    job_stage(0, 4)

    @pl.loop(0, NT)
    def _(e):
        message_slope(e)

    gradient(768, [(hid, 0, NT)], [(pool4, 0)])
    job_stage(1, 0)
    gradient(1280, [(nv, 0, NT)], [(pool0, 0)])
    job_stage(2, 0)
    job_stage(1, 1)
    job_stage(0, 5)
    gradient(1792, [(agg, 0, NT)], [(pool0, 0)])
    job_stage(3, 0)
    job_stage(2, 1)
    gradient(2304, [(nv, 0, NT), (halo, 0, NT)], [(mbuf, 0), (mbuf, NT)])
    job_stage(4, 0)
    job_stage(3, 1)
    job_stage(1, 2)
    job_stage(0, 6)

    @pl.loop(0, NT // GROUP)
    def _(g):
        put_rows(g2f, g * GROUP, rows_of(g2f, g * GROUP) + dot_nt(rows_of(mbuf, g * GROUP), wm[...]))

    part_out = pltpu.make_async_copy(g2f, part_hbm, out_sem.at[0])
    part_out.start()
    job_stage(4, 1)
    for step in range(2, 8):
        if step < 7:
            job_stage(1, step + 1)
        for j in (2, 3, 4):
            job_stage(j, step)
    job_stage(0, 7)
    part_out.wait()
    for d in range(4):
        when(back_has[d], lambda d=d: back_copy(d).wait_send())
        when(back_from[d], lambda d=d: back_copy(d).wait_recv())


def finish(sizes, send_ref, part_ref, back_ref, m_ref, u_ref, a_ref, o_ref, d_ref, h_ref,
           latent_ref, msg_ref, upd_ref, agg_ref, out_ref, dec_ref, head_ref):
    r = lax.axis_index("row")
    step = pl.program_id(0)
    per = part_ref.shape[0]
    for i in range(per):
        latent_ref[i] = part_ref[i]
    for d in range(4):
        there = (r < sizes["rows"] - 1, r > 0, None, None)[d]
        for b in range(4):
            local = send_ref[0, d, b] - step * per
            hit = (local >= 0) & (local < per)
            if there is not None:
                hit = hit & there

            @pl.when(hit)
            def _(local=local, a=d * 4 + b):
                latent_ref[local] = latent_ref[local] + back_ref[a].astype(F32)

    for src, dst in ((m_ref, msg_ref), (u_ref, upd_ref), (a_ref, agg_ref), (o_ref, out_ref), (d_ref, dec_ref), (h_ref, head_ref)):
        dst[:, :HALF] = src[0].astype(F32)
        dst[:, HALF:] = src[1].astype(F32)


def on_device(
    sizes, nodes, send_list, adj_index, adj_weight, dec_send, dec_index, dec_weight, hidden_mask, target,
    w_msg, w_update, w_aggregate, w_output, w_decode, w_head,
):
    n = sizes["n"]
    tiles = lambda count, dtype=BF16: pltpu.VMEM((count, TILE, D), dtype)
    any_spec = pl.BlockSpec(memory_space=pl.ANY)
    smem = pl.BlockSpec(memory_space=pltpu.SMEM)
    scratch = [
        tiles(NT), tiles(NT),
        pltpu.VMEM((NT * K, TILE, TILE), BF16), pltpu.VMEM((NT * KD, TILE, TILE), BF16),
        pltpu.VMEM((NT, OUTC, TILE), BF16),
        *[pltpu.VMEM((D, D), BF16)] * 5, pltpu.VMEM((OUTC, D), BF16),
        tiles(2 * NE), tiles(NE), tiles(NT, F32),
        tiles(NT), tiles(NT), tiles(NT),
        tiles(8), tiles(8), pltpu.VMEM((OUTC, SLOTS * TILE), BF16),
        tiles(NT), tiles(NT), tiles(NE), tiles(NT),
        pltpu.VMEM((TILE, D), F32),
        pltpu.VMEM((GRAD_F32, D), F32),
        pltpu.VMEM((GRAD_ROWS, HALF), BF16), pltpu.VMEM((GRAD_ROWS, HALF), BF16),
        pltpu.VMEM((n - 1, GRAD_ROWS // n, HALF), BF16), pltpu.VMEM((GRAD_ROWS // n, HALF), BF16),
        pltpu.VMEM((n - 1, GRAD_ROWS // n**2, HALF), BF16), pltpu.VMEM((n, GRAD_ROWS // n**2, HALF), BF16),
        pltpu.VMEM((24, 128), jnp.int32), pltpu.SMEM((24, 128), jnp.int32),
        pltpu.SemaphoreType.DMA((9 + NT,)), pltpu.SemaphoreType.DMA((2,)), pltpu.SemaphoreType.DMA((1,)),
        *[pltpu.SemaphoreType.DMA((4,))] * 2,
        *[pltpu.SemaphoreType.DMA((2,))] * 4,
        *[pltpu.SemaphoreType.DMA((4,))] * 2,
        *[pltpu.SemaphoreType.DMA((len(JOBS), JOB_SEMS))] * 2,
        pltpu.SemaphoreType.DMA((len(JOBS),)),
    ]
    part, back, grads = pl.pallas_call(
        functools.partial(kernel, sizes),
        out_shape=(
            jax.ShapeDtypeStruct((NT, TILE, D), F32),
            jax.ShapeDtypeStruct((NT, TILE, D), BF16),
            jax.ShapeDtypeStruct((CORES, GRAD_ROWS, HALF), BF16),
        ),
        in_specs=[smem] * 5 + [any_spec] * 10,
        out_specs=(any_spec,) * 3,
        scratch_shapes=scratch,
        compiler_params=pltpu.CompilerParams(
            collective_id=0, has_side_effects=True, vmem_limit_bytes=62 * 1024 * 1024
        ),
        name="mesh_step",
    )(
        send_list, adj_index.transpose(0, 2, 1), dec_send, dec_index.transpose(2, 0, 1), hidden_mask,
        nodes.reshape(NT, TILE, D),
        adj_weight.reshape(NT * K, TILE, TILE),
        dec_weight.reshape(NT * KD, TILE, TILE),
        target.T,
        w_msg, w_update, w_aggregate, w_output, w_decode, w_head.T,
    )
    steps = 8
    block = D // steps

    def rows_spec(at, size=block):
        return pl.BlockSpec((CORES, size, HALF), lambda i, s: (0, at // size + i, 0))

    square = pl.BlockSpec((block, D), lambda i, s: (i, 0))
    f32 = lambda *shape: jax.ShapeDtypeStruct(shape, F32)
    outs = pl.pallas_call(
        functools.partial(finish, sizes),
        out_shape=(f32(NT, TILE, D), *[f32(D, D)] * 5, f32(OUTC, D)),
        grid_spec=pltpu.PrefetchScalarGridSpec(
            num_scalar_prefetch=1,
            grid=(steps,),
            in_specs=[
                pl.BlockSpec((NT // steps, TILE, D), lambda i, s: (i, 0, 0)),
                pl.BlockSpec((NT, TILE, D), lambda i, s: (0, 0, 0)),
                rows_spec(2304), rows_spec(1280), rows_spec(1792), rows_spec(768), rows_spec(0),
                rows_spec(512, HALF // steps),
            ],
            out_specs=(
                pl.BlockSpec((NT // steps, TILE, D), lambda i, s: (i, 0, 0)),
                *[square] * 5,
                pl.BlockSpec((HALF // steps, D), lambda i, s: (i, 0)),
            ),
        ),
        compiler_params=pltpu.CompilerParams(vmem_limit_bytes=60 * 1024 * 1024),
        name="finish",
    )(send_list, part, back, grads, grads, grads, grads, grads, grads)
    latent, msg, upd, agg, out, dec, head = outs
    return latent.reshape(NT * TILE, D), msg, upd, agg, out, dec, head.T


def solution(mesh):
    rows, cols = mesh.shape["row"], mesh.shape["col"]
    sizes = dict(axes_of(rows, cols), rows=rows, cols=cols)
    both = ("row", "col")
    return jax.shard_map(
        functools.partial(on_device, sizes),
        mesh=mesh,
        in_specs=(
            P(both, None),
            P(both, None, None),
            P(both, None, None),
            P(both, None, None, None),
            P(both, None, None),
            P(both, None, None),
            P(both, None, None, None),
            P(both, None),
            P(both, None),
            *[P()] * 6,
        ),
        out_specs=(P(both, None), *[P()] * 6),
        check_vma=False,
    )
```

profile of v0, /device:TPU:1, one launch (start us, length us, event | category | flops | bytes accessed | tf_op | source)
XLA Modules:
  0.0 134.8 jit_solution(2557507231994335279)
XLA Ops:
  0.6 123.3 %mesh_step.1 = (f32[16,128,512]{2,1,0:T(8,128)}, bf16[16,128,512]{2,1,0:T(8,128)(2,1)}, bf16[2,2816,256]{2,1,0:T(8,128)(2,1)}) custom-call(s32[1,4,4]{2,1,0:T(4,128)} %send_ref.3, s32[1,4,16]{2,1,0:T(4,128)} %bitcast.14, s32[1,2,4]{2,1,0:T(2,128)} %dsend_ref.1, s32[3,1,16]{2,1,0:T(1,128)} %bitcast.15, s32[1,16]{1,0:T(1,128)} %mask_ref.1, ...), custom_call_target="tpu_custom_call" | custom-call | tf_op jit(solution)/shard_map/mesh_step/pallas_call | solution.py:614
  124.0 10.7 %finish.1 = (f32[16,128,512]{2,1,0:T(8,128)}, f32[512,512]{1,0:T(8,128)}, f32[512,512]{1,0:T(8,128)}, f32[512,512]{1,0:T(8,128)}, f32[512,512]{1,0:T(8,128)}, /*index=5*/f32[512,512]{1,0:T(8,128)}, f32[227,512]{1,0:T(8,128)}) custom-call(s32[1,4,4]{2,1,0:T(4,128)} %send_ref.3, f32[16,128,512]{2,1,0:T(8,128)} %get-tuple-element.17.part_ref, ...), custom_call_target="tpu_custom_call" | custom-call | tf_op jit(solution)/shard_map/finish/pallas_call | solution.py:644
where the time goes:
time: 135 us
  Pallas kernels  134 us (99%)
    pallas_call x1, Pallas kernels, on_device(): pl.pallas_call(functools.partial(kernel, sizes), out_shape=(jax.ShapeDtyp...  123 us
    pallas_call x1, Pallas kernels, on_device(): pl.pallas_call(functools.partial(finish, sizes), out_shape=(f32(NT, TILE,...  10.7 us

commit v1 on v0

--- a/solution.py
+++ b/solution.py
@@ -31,7 +31,8 @@
     (768, 512, ("y", "x", "z")),
     (1280, 512, ("x", "z", "y")),
     (1792, 512, ("z", "x", "y")),
-    (2304, 512, ("y", "z", "x")),
+    (2304, 256, ("y", "z", "x")),
+    (2560, 256, ("z", "y", "x")),
 )
 GRAD_ROWS = 2816
 GRAD_F32 = 2304
@@ -104,12 +105,13 @@
     send_ref, adj_ref, dsend_ref, didx_ref, mask_ref,
     nodes_hbm, adjw_hbm, decw_hbm, target_hbm,
     wm_hbm, wu_hbm, wa_hbm, wo_hbm, wd_hbm, wh_hbm,
-    part_hbm, back_hbm, grads_hbm,
+    lat_hbm, grads_hbm,
     nv, halo, adjw, decw, target, wm, wu, wa, wo, wd, wh,
     pref, msl, g2f, agg, hid, usl, redge, rgin, err, pool0, pool1, mbuf, pool4, acc,
     gbuf, cs, cr, r1, s2, r2, x4,
-    plan_v, plan,
+    rel, backns, plan_v, plan,
     in_sems, plan_sem, out_sem, halo_s, halo_r, edge_s, edge_r, rg_s, rg_r, hg_s, hg_r, job_s, job_r, job_l,
+    hop_s, hop_r, fwd_s, fwd_r,
 ):
     nrow, ncol, nx, ny, nzl = sizes["rows"], sizes["cols"], sizes["x"], sizes["y"], sizes["zl"]
     nzh, n = sizes["zh"], sizes["n"]
@@ -137,6 +139,11 @@
     south = (r + 1, c)
     has_north = r > 0
     has_south = r < nrow - 1
+    split = nzh == 2
+    flip = ((1 - zl) * ny + y) * CORES + core
+    relays = ((nx - 1, nx - 1, nx, 0), (nrow - 1, nx - 1, nx, 1), (nx, nx, nx - 1, 0), (0, nx, nx - 1, 1)) if split else ()
+    to_south = has_south & (r != nx - 1) if split else has_south
+    to_north = has_north & (r != nx) if split else has_north
 
     loads = [
         pltpu.make_async_copy(src, dst, in_sems.at[i])
@@ -148,7 +155,7 @@
             )
         )
     ]
-    for load in loads:
+    for load in loads[:3]:
         load.start()
 
     barrier = pltpu.get_barrier_semaphore()
@@ -172,6 +179,19 @@
     def _():
         greet(south)
 
+    extra = jnp.where(has_north, 1, 0) + jnp.where(has_south, 1, 0)
+    for row, _, target_row, _ in relays:
+
+        @pl.when(r == row)
+        def _(target_row=target_row):
+            greet((target_row, flip))
+
+        @pl.when(r == target_row)
+        def _(row=row):
+            greet((row, flip))
+
+        extra = extra + jnp.where(r == row, 1, 0) + jnp.where(r == target_row, 1, 0)
+
     def send(src, dst, ssem, rsem, device):
         return pltpu.make_async_remote_copy(
             src_ref=src, dst_ref=dst, send_sem=ssem, recv_sem=rsem, device_id=device, device_id_type=MESH
@@ -181,11 +201,12 @@
     for d in range(4):
         for b in range(4):
             pool1[d * 4 + b] = nv[send_ref[0, d, b]]
-    pl.semaphore_wait(barrier, greeted + jnp.where(has_north, 1, 0) + jnp.where(has_south, 1, 0))
+    pl.semaphore_wait(barrier, greeted + extra)
 
     halo_to = (south, north, east, west)
-    halo_has = (has_south, has_north, None, None)
-    from_has = (has_north, has_south, None, None)
+    halo_has = (to_south, to_north, None, None)
+    from_has = (to_north, to_south, None, None)
+    no_from = (jnp.logical_not(has_north), jnp.logical_not(has_south))
 
     def when(condition, body):
         if condition is None:
@@ -197,8 +218,60 @@
         part = pl.ds(d * 4, 4)
         return send(pool1.at[part], halo.at[part], halo_s.at[d], halo_r.at[d], halo_to[d])
 
+    def hop_copy(turn, half, i, start, row):
+        return send(
+            pool1.at[start + half * 2 + i], rel.at[turn * 2 + i], hop_s.at[turn, half * 2 + i], hop_r.at[turn, i], (row, flip)
+        )
+
+    def forward_copy(turn, half, i, dst, start, row):
+        return send(
+            rel.at[turn * 2 + i], dst.at[start + half * 2 + i], fwd_s.at[turn, i], fwd_r.at[turn, half * 2 + i], (row, flip)
+        )
+
+    def hops(turn, starts, act):
+        for row, source, _, half in relays:
+            start = starts[0] if source == nx - 1 else starts[1]
+
+            @pl.when(r == source)
+            def _(row=row, half=half, start=start):
+                for i in range(2):
+                    act(hop_copy(turn, half, i, start, row))
+
+    def forward(turn, i, dst, starts, begin):
+        for row, source, target_row, half in relays:
+            start = starts[0] if source == nx - 1 else starts[1]
+
+            @pl.when(r == row)
+            def _(target_row=target_row, half=half, start=start):
+                copy = forward_copy(turn, half, i, dst, start, target_row)
+                if begin:
+                    hop_copy(turn, half, i, 0, 0).wait_recv()
+                    copy.start()
+                else:
+                    copy.wait_send()
+
+    def arrivals(turn, dst, starts):
+        for row, source, target_row, half in relays:
+            start = starts[0] if source == nx - 1 else starts[1]
+
+            @pl.when(r == target_row)
+            def _(row=row, half=half, start=start):
+                for i in range(2):
+                    forward_copy(turn, half, i, dst, start, row).wait_recv()
+
     for d in range(4):
         when(halo_has[d], lambda d=d: halo_copy(d).start())
+        if d == 1:
+            hops(0, (0, 4), lambda copy: copy.start())
+    for load in loads[3:]:
+        load.start()
+
+    for d in range(2):
+
+        @pl.when(no_from[d])
+        def _(d=d):
+            halo[pl.ds(d * 4, 4)] = jnp.zeros((4, TILE, D), BF16)
+            backns[pl.ds(4 - d * 4, 4)] = jnp.zeros((4, TILE, D), BF16)
 
     def messages(xs, at):
         pre = dot(xs, wm[...])
@@ -215,6 +288,8 @@
         messages(xs, g * GROUP)
         put_rows(g2f, g * GROUP, dot(xs, wu[...]))
 
+    forward(0, 0, halo, (0, 4), True)
+
     def write_plan(at, rows):
         for i, row in enumerate(rows):
             plan_v[at + i : at + i + 1, :] = row
@@ -222,6 +297,7 @@
     write_plan(0, sort_plan([adj_ref[0, k, t] for t in range(NT) for k in range(K)], per=K))
     write_plan(6, sort_plan([dsend_ref[0, d, s] for d in range(2) for s in range(4)])[:4])
     write_plan(10, sort_plan([1 - mask_ref[0, g] for g in range(NT)])[:1])
+    write_plan(11, sort_plan([send_ref[0, d, b] for d in range(4) for b in range(4)])[:4])
     first = pltpu.make_async_copy(plan_v.at[pl.ds(0, 16)], plan.at[pl.ds(0, 16)], plan_sem.at[0])
     first.start()
     first.wait()
@@ -232,14 +308,11 @@
     second.start()
     second.wait()
 
+    forward(0, 1, halo, (0, 4), True)
     for d in (3, 2, 0, 1):
         when(from_has[d], lambda d=d: halo_copy(d).wait_recv())
-        if from_has[d] is not None:
-
-            @pl.when(jnp.logical_not(from_has[d]))
-            def _(d=d):
-                halo[pl.ds(d * 4, 4)] = jnp.zeros((4, TILE, D), BF16)
-
+        if d == 0:
+            arrivals(0, halo, (0, 4))
         messages(rows_of(halo, d * 4), NT + d * 4)
 
     for i in (3, 4, 5):
@@ -264,6 +337,7 @@
 
     for d in range(4):
         when(halo_has[d], lambda d=d: halo_copy(d).wait_send())
+    hops(0, (0, 4), lambda copy: copy.wait_send())
     for d in range(2):
         for s in range(4):
             pref[NE + d * 4 + s] = pref[dsend_ref[0, d, s]]
@@ -303,10 +377,11 @@
         put_rows(mbuf, g * GROUP, dslope)
         put_rows(pool4, g * GROUP, dot_nt(dslope, wd[...]).astype(BF16))
 
-    def spread(at, edges, weight, source):
-        acc[...] = jnp.zeros((TILE, D), F32)
-
-        @pl.loop(0, edges // GROUP)
+    def spread(at, first_edge, last_edge, weight, source):
+        if first_edge == 0:
+            acc[...] = jnp.zeros((TILE, D), F32)
+
+        @pl.loop(first_edge // GROUP, last_edge // GROUP)
         def _(h):
             total = acc[...]
             for i in range(GROUP):
@@ -318,7 +393,7 @@
     def spread_of(at, tile):
         return plan[at + 3, tile].astype(F32) * pref[plan[at + 2, tile]].astype(F32)
 
-    spread(16, DEC_EDGES, decw, pool4)
+    spread(16, 0, DEC_EDGES, decw, pool4)
     for e in range(8):
         pref[48 + e] = spread_of(16, NT + e).astype(BF16)
     returns = [
@@ -451,16 +526,15 @@
             for item in back_core(j):
                 item.wait()
 
-    def gradient(at, left, right):
-        for n in range(2):
-            lanes = slice(n * HALF, (n + 1) * HALF)
+    def gradient(at, left, right, halves=(0, 1)):
+        for half in halves:
+            lanes = slice(half * HALF, (half + 1) * HALF)
             total = None
             for (lref, lat, count), (rref, rat) in zip(left, right):
-                lhs = lref[pl.ds(lat, count)].reshape(count * TILE, D)
-                rhs = rref[pl.ds(rat, count), :, lanes].reshape(count * TILE, HALF)
-                term = dot_tn(lhs, rhs)
+                lhs = lref[pl.ds(lat, count), :, lanes].reshape(count * TILE, HALF)
+                term = dot_tn(lhs, rows_of(rref, rat, count))
                 total = term if total is None else total + term
-            gbuf[pl.ds(at % GRAD_F32, D), lanes] = total
+            gbuf[pl.ds(at % GRAD_F32 + half * HALF, HALF)] = total
 
     gradient(0, [(pool0, 0, SLOTS)], [(mbuf, 0)])
     q_rows = pool1[pl.ds(0, SLOTS)].reshape(SLOTS * TILE, D)
@@ -484,6 +558,8 @@
         pool4[t] = value.astype(BF16)
 
     job_stage(0, 1)
+    gradient(768, [(hid, 0, NT)], [(pool4, 0)])
+    job_stage(1, 0)
 
     @pl.loop(0, NT // GROUP)
     def _(g):
@@ -494,19 +570,28 @@
         put_rows(pool1, g * GROUP, dot_nt(slope, wa[...]).astype(BF16))
 
     job_stage(0, 2)
-    spread(0, ADJ_EDGES, adjw, pool1)
+    job_stage(1, 1)
+    gradient(1280, [(nv, 0, NT)], [(pool0, 0)])
+    job_stage(2, 0)
+    gradient(1792, [(agg, 0, NT)], [(pool0, 0)])
+    job_stage(3, 0)
+    job_stage(2, 1)
+    spread(0, 0, ADJ_EDGES // 2, adjw, pool1)
     job_stage(0, 3)
+    job_stage(3, 1)
+    job_stage(1, 2)
+    spread(0, ADJ_EDGES // 2, ADJ_EDGES, adjw, pool1)
 
     def message_slope(e):
         mbuf[e] = (spread_of(0, e) * msl[e].astype(F32)).astype(BF16)
 
     back_to = (north, south, west, east)
-    back_has = (has_north, has_south, None, None)
-    back_from = (has_south, has_north, None, None)
+    back_has = (to_north, to_south, None, None)
+    back_from = (to_south, to_north, None, None)
 
     def back_copy(d):
-        part = pl.ds(d * 4, 4)
-        return send(pool1.at[part], back_hbm.at[part], hg_s.at[d], hg_r.at[d], back_to[d])
+        dst = (backns.at[pl.ds(0, 4)], backns.at[pl.ds(4, 4)], redge.at[pl.ds(0, 4)], redge.at[pl.ds(4, 4)])[d]
+        return send(pool1.at[pl.ds(d * 4, 4)], dst, hg_s.at[d], hg_r.at[d], back_to[d])
 
     for d in range(4):
 
@@ -516,67 +601,91 @@
 
         put_rows(pool1, d * 4, dot_nt(rows_of(mbuf, NT + d * 4), wm[...]).astype(BF16))
         when(back_has[d], lambda d=d: back_copy(d).start())
+        if d == 1:
+            hops(1, (4, 0), lambda copy: copy.start())
 
     job_stage(0, 4)
+    job_stage(2, 2)
 
     @pl.loop(0, NT)
     def _(e):
         message_slope(e)
 
-    gradient(768, [(hid, 0, NT)], [(pool4, 0)])
-    job_stage(1, 0)
-    gradient(1280, [(nv, 0, NT)], [(pool0, 0)])
-    job_stage(2, 0)
-    job_stage(1, 1)
+    job_stage(1, 3)
+    job_stage(3, 2)
+    left, right = [(nv, 0, NT), (halo, 0, NT)], [(mbuf, 0), (mbuf, NT)]
+    gradient(2304, left, right, (0,))
+    job_stage(4, 0)
+    forward(1, 0, backns, (4, 0), True)
     job_stage(0, 5)
-    gradient(1792, [(agg, 0, NT)], [(pool0, 0)])
-    job_stage(3, 0)
-    job_stage(2, 1)
-    gradient(2304, [(nv, 0, NT), (halo, 0, NT)], [(mbuf, 0), (mbuf, NT)])
-    job_stage(4, 0)
-    job_stage(3, 1)
-    job_stage(1, 2)
-    job_stage(0, 6)
+    job_stage(2, 3)
+    gradient(2304, left, right, (1,))
+    job_stage(5, 0)
+    job_stage(4, 1)
+    forward(1, 1, backns, (4, 0), True)
+    job_stage(3, 3)
+    job_stage(1, 4)
 
     @pl.loop(0, NT // GROUP)
     def _(g):
         put_rows(g2f, g * GROUP, rows_of(g2f, g * GROUP) + dot_nt(rows_of(mbuf, g * GROUP), wm[...]))
 
-    part_out = pltpu.make_async_copy(g2f, part_hbm, out_sem.at[0])
-    part_out.start()
-    job_stage(4, 1)
-    for step in range(2, 8):
-        if step < 7:
-            job_stage(1, step + 1)
-        for j in (2, 3, 4):
-            job_stage(j, step)
-    job_stage(0, 7)
-    part_out.wait()
+    job_stage(5, 1)
+    job_stage(0, 6)
+    job_stage(2, 4)
+    job_stage(4, 2)
+    job_stage(3, 4)
+    job_stage(1, 5)
+    job_stage(5, 2)
+    job_stage(2, 5)
+    job_stage(4, 3)
+    job_stage(3, 5)
+    job_stage(5, 3)
+    job_stage(1, 6)
+    for d in range(4):
+        when(back_from[d], lambda d=d: back_copy(d).wait_recv())
+    arrivals(1, backns, (4, 0))
+    for e in range(8):
+        pref[e] = backns[e]
+        pref[8 + e] = redge[e]
+    job_stage(4, 4)
+    job_stage(5, 4)
+    total = None
+    for p in range(16):
+        arrived = pref[plan[11, p]].astype(F32)
+        total = arrived if total is None else arrived + plan[12, p].astype(F32) * total
+        pref[16 + p] = total.astype(BF16)
+
+    @pl.loop(0, NT)
+    def _(t):
+        value = g2f[t] + plan[14, t].astype(F32) * pref[16 + plan[13, t]].astype(F32)
+        agg[t] = value.astype(BF16)
+
+    lat_out = pltpu.make_async_copy(agg, lat_hbm, out_sem.at[0])
+    lat_out.start()
+    for stage in range(5, 7):
+        for j in (4, 5):
+            job_stage(j, stage)
+        if stage == 5:
+            job_stage(2, 6)
+            job_stage(3, 6)
+    for j in range(len(JOBS)):
+        job_stage(j, 7)
+    lat_out.wait()
     for d in range(4):
         when(back_has[d], lambda d=d: back_copy(d).wait_send())
-        when(back_from[d], lambda d=d: back_copy(d).wait_recv())
-
-
-def finish(sizes, send_ref, part_ref, back_ref, m_ref, u_ref, a_ref, o_ref, d_ref, h_ref,
+    hops(1, (4, 0), lambda copy: copy.wait_send())
+    for turn in range(2):
+        for i in range(2):
+            forward(turn, i, (halo, backns)[turn], (0, 4), False)
+
+
+def finish(lat_ref, m_ref, u_ref, a_ref, o_ref, d_ref, h_ref,
            latent_ref, msg_ref, upd_ref, agg_ref, out_ref, dec_ref, head_ref):
-    r = lax.axis_index("row")
-    step = pl.program_id(0)
-    per = part_ref.shape[0]
-    for i in range(per):
-        latent_ref[i] = part_ref[i]
-    for d in range(4):
-        there = (r < sizes["rows"] - 1, r > 0, None, None)[d]
-        for b in range(4):
-            local = send_ref[0, d, b] - step * per
-            hit = (local >= 0) & (local < per)
-            if there is not None:
-                hit = hit & there
-
-            @pl.when(hit)
-            def _(local=local, a=d * 4 + b):
-                latent_ref[local] = latent_ref[local] + back_ref[a].astype(F32)
-
-    for src, dst in ((m_ref, msg_ref), (u_ref, upd_ref), (a_ref, agg_ref), (o_ref, out_ref), (d_ref, dec_ref), (h_ref, head_ref)):
+    latent_ref[...] = lat_ref[...].astype(F32)
+    for src, dst in (
+        (m_ref, msg_ref), (u_ref, upd_ref), (a_ref, agg_ref), (o_ref, out_ref), (d_ref, dec_ref), (h_ref, head_ref),
+    ):
         dst[:, :HALF] = src[0].astype(F32)
         dst[:, HALF:] = src[1].astype(F32)
 
@@ -603,6 +712,7 @@
         pltpu.VMEM((GRAD_ROWS, HALF), BF16), pltpu.VMEM((GRAD_ROWS, HALF), BF16),
         pltpu.VMEM((n - 1, GRAD_ROWS // n, HALF), BF16), pltpu.VMEM((GRAD_ROWS // n, HALF), BF16),
         pltpu.VMEM((n - 1, GRAD_ROWS // n**2, HALF), BF16), pltpu.VMEM((n, GRAD_ROWS // n**2, HALF), BF16),
+        tiles(4), tiles(8),
         pltpu.VMEM((24, 128), jnp.int32), pltpu.SMEM((24, 128), jnp.int32),
         pltpu.SemaphoreType.DMA((9 + NT,)), pltpu.SemaphoreType.DMA((2,)), pltpu.SemaphoreType.DMA((1,)),
         *[pltpu.SemaphoreType.DMA((4,))] * 2,
@@ -610,16 +720,17 @@
         *[pltpu.SemaphoreType.DMA((4,))] * 2,
         *[pltpu.SemaphoreType.DMA((len(JOBS), JOB_SEMS))] * 2,
         pltpu.SemaphoreType.DMA((len(JOBS),)),
+        pltpu.SemaphoreType.DMA((2, 4)), pltpu.SemaphoreType.DMA((2, 2)),
+        pltpu.SemaphoreType.DMA((2, 2)), pltpu.SemaphoreType.DMA((2, 4)),
     ]
-    part, back, grads = pl.pallas_call(
+    lat, grads = pl.pallas_call(
         functools.partial(kernel, sizes),
         out_shape=(
-            jax.ShapeDtypeStruct((NT, TILE, D), F32),
             jax.ShapeDtypeStruct((NT, TILE, D), BF16),
             jax.ShapeDtypeStruct((CORES, GRAD_ROWS, HALF), BF16),
         ),
         in_specs=[smem] * 5 + [any_spec] * 10,
-        out_specs=(any_spec,) * 3,
+        out_specs=(any_spec,) * 2,
         scratch_shapes=scratch,
         compiler_params=pltpu.CompilerParams(
             collective_id=0, has_side_effects=True, vmem_limit_bytes=62 * 1024 * 1024
@@ -637,31 +748,20 @@
     block = D // steps
 
     def rows_spec(at, size=block):
-        return pl.BlockSpec((CORES, size, HALF), lambda i, s: (0, at // size + i, 0))
-
-    square = pl.BlockSpec((block, D), lambda i, s: (i, 0))
+        return pl.BlockSpec((CORES, size, HALF), lambda i: (0, at // size + i, 0))
+
+    latents = pl.BlockSpec((NT // steps, TILE, D), lambda i: (i, 0, 0))
+    square = pl.BlockSpec((block, D), lambda i: (i, 0))
     f32 = lambda *shape: jax.ShapeDtypeStruct(shape, F32)
     outs = pl.pallas_call(
-        functools.partial(finish, sizes),
+        finish,
         out_shape=(f32(NT, TILE, D), *[f32(D, D)] * 5, f32(OUTC, D)),
-        grid_spec=pltpu.PrefetchScalarGridSpec(
-            num_scalar_prefetch=1,
-            grid=(steps,),
-            in_specs=[
-                pl.BlockSpec((NT // steps, TILE, D), lambda i, s: (i, 0, 0)),
-                pl.BlockSpec((NT, TILE, D), lambda i, s: (0, 0, 0)),
-                rows_spec(2304), rows_spec(1280), rows_spec(1792), rows_spec(768), rows_spec(0),
-                rows_spec(512, HALF // steps),
-            ],
-            out_specs=(
-                pl.BlockSpec((NT // steps, TILE, D), lambda i, s: (i, 0, 0)),
-                *[square] * 5,
-                pl.BlockSpec((HALF // steps, D), lambda i, s: (i, 0)),
-            ),
-        ),
+        grid=(steps,),
+        in_specs=[latents, *(rows_spec(at) for at in (2304, 1280, 1792, 768, 0)), rows_spec(512, HALF // steps)],
+        out_specs=(latents, *[square] * 5, pl.BlockSpec((HALF // steps, D), lambda i: (i, 0))),
         compiler_params=pltpu.CompilerParams(vmem_limit_bytes=60 * 1024 * 1024),
         name="finish",
-    )(send_list, part, back, grads, grads, grads, grads, grads, grads)
+    )(lat, grads, grads, grads, grads, grads, grads)
     latent, msg, upd, agg, out, dec, head = outs
     return latent.reshape(NT * TILE, D), msg, upd, agg, out, dec, head.T
 

time: 135 us -> 136 us (level)
    pallas_call x1, Pallas kernels: 123 us -> 127 us  [on_device(): pl.pallas_call(functools.partial(kernel, sizes), out_shape=(jax.ShapeDtyp...]
    pallas_call x1, Pallas kernels: 10.7 us -> 7.56 us  [on_device(): pl.pallas_call(finish, out_shape=(f32(NT, TILE, D), *[f32(D, D)] * 5, f32...]
where the time goes in v1:
time: 136 us
  Pallas kernels  135 us (99%)
    pallas_call x1, Pallas kernels, on_device(): pl.pallas_call(functools.partial(kernel, sizes), out_shape=(jax.ShapeDtyp...  127 us
    pallas_call x1, Pallas kernels, on_device(): pl.pallas_call(finish, out_shape=(f32(NT, TILE, D), *[f32(D, D)] * 5, f32...  7.56 us

profile of v1, /device:TPU:1, one launch (start us, length us, event | category | flops | bytes accessed | tf_op | source)
XLA Modules:
  0.0 135.8 jit_solution(13488586383501466941)
XLA Ops:
  0.6 127.4 %mesh_step.1 = (bf16[16,128,512]{2,1,0:T(8,128)(2,1)}, bf16[2,2816,256]{2,1,0:T(8,128)(2,1)}) custom-call(s32[1,4,4]{2,1,0:T(4,128)} %send_ref.1, s32[1,4,16]{2,1,0:T(4,128)} %bitcast.14, s32[1,2,4]{2,1,0:T(2,128)} %dsend_ref.1, s32[3,1,16]{2,1,0:T(1,128)} %bitcast.15, s32[1,16]{1,0:T(1,128)} %mask_ref.1, bf16[16,128,512]{2,1,0:T(8,128)(2,1)} %bitcast.9, ...), custom_call_target="tpu_custom_call" | custom-call | tf_op jit(solution)/shard_map/mesh_step/pallas_call | solution.py:726
  128.1 7.6 %finish.1 = (f32[16,128,512]{2,1,0:T(8,128)}, f32[512,512]{1,0:T(8,128)}, f32[512,512]{1,0:T(8,128)}, f32[512,512]{1,0:T(8,128)}, f32[512,512]{1,0:T(8,128)}, /*index=5*/f32[512,512]{1,0:T(8,128)}, f32[227,512]{1,0:T(8,128)}) custom-call(bf16[16,128,512]{2,1,0:T(8,128)(2,1)} %get-tuple-element.16.lat_ref, ...), custom_call_target="tpu_custom_call" | custom-call | tf_op jit(solution)/shard_map/finish/pallas_call | solution.py:756

commit v2 on v1

--- a/solution.py
+++ b/solution.py
@@ -69,6 +69,10 @@
 
 def put_rows(ref, start, value, count=GROUP):
     ref[pl.ds(start, count)] = value.reshape(count, TILE, value.shape[-1])
+
+
+def outer_first(value, inner, outer):
+    return jnp.where(value >= inner, value - inner, value + outer)
 
 
 def sort_plan(values, blocks=None, per=1):
@@ -109,9 +113,8 @@
     nv, halo, adjw, decw, target, wm, wu, wa, wo, wd, wh,
     pref, msl, g2f, agg, hid, usl, redge, rgin, err, pool0, pool1, mbuf, pool4, acc,
     gbuf, cs, cr, r1, s2, r2, x4,
-    rel, backns, plan_v, plan,
+    backns, plan_v, plan,
     in_sems, plan_sem, out_sem, halo_s, halo_r, edge_s, edge_r, rg_s, rg_r, hg_s, hg_r, job_s, job_r, job_l,
-    hop_s, hop_r, fwd_s, fwd_r,
 ):
     nrow, ncol, nx, ny, nzl = sizes["rows"], sizes["cols"], sizes["x"], sizes["y"], sizes["zl"]
     nzh, n = sizes["zh"], sizes["n"]
@@ -139,11 +142,6 @@
     south = (r + 1, c)
     has_north = r > 0
     has_south = r < nrow - 1
-    split = nzh == 2
-    flip = ((1 - zl) * ny + y) * CORES + core
-    relays = ((nx - 1, nx - 1, nx, 0), (nrow - 1, nx - 1, nx, 1), (nx, nx, nx - 1, 0), (0, nx, nx - 1, 1)) if split else ()
-    to_south = has_south & (r != nx - 1) if split else has_south
-    to_north = has_north & (r != nx) if split else has_north
 
     loads = [
         pltpu.make_async_copy(src, dst, in_sems.at[i])
@@ -180,17 +178,6 @@
         greet(south)
 
     extra = jnp.where(has_north, 1, 0) + jnp.where(has_south, 1, 0)
-    for row, _, target_row, _ in relays:
-
-        @pl.when(r == row)
-        def _(target_row=target_row):
-            greet((target_row, flip))
-
-        @pl.when(r == target_row)
-        def _(row=row):
-            greet((row, flip))
-
-        extra = extra + jnp.where(r == row, 1, 0) + jnp.where(r == target_row, 1, 0)
 
     def send(src, dst, ssem, rsem, device):
         return pltpu.make_async_remote_copy(
@@ -204,8 +191,8 @@
     pl.semaphore_wait(barrier, greeted + extra)
 
     halo_to = (south, north, east, west)
-    halo_has = (to_south, to_north, None, None)
-    from_has = (to_north, to_south, None, None)
+    halo_has = (has_south, has_north, None, None)
+    from_has = (has_north, has_south, None, None)
     no_from = (jnp.logical_not(has_north), jnp.logical_not(has_south))
 
     def when(condition, body):
@@ -218,51 +205,8 @@
         part = pl.ds(d * 4, 4)
         return send(pool1.at[part], halo.at[part], halo_s.at[d], halo_r.at[d], halo_to[d])
 
-    def hop_copy(turn, half, i, start, row):
-        return send(
-            pool1.at[start + half * 2 + i], rel.at[turn * 2 + i], hop_s.at[turn, half * 2 + i], hop_r.at[turn, i], (row, flip)
-        )
-
-    def forward_copy(turn, half, i, dst, start, row):
-        return send(
-            rel.at[turn * 2 + i], dst.at[start + half * 2 + i], fwd_s.at[turn, i], fwd_r.at[turn, half * 2 + i], (row, flip)
-        )
-
-    def hops(turn, starts, act):
-        for row, source, _, half in relays:
-            start = starts[0] if source == nx - 1 else starts[1]
-
-            @pl.when(r == source)
-            def _(row=row, half=half, start=start):
-                for i in range(2):
-                    act(hop_copy(turn, half, i, start, row))
-
-    def forward(turn, i, dst, starts, begin):
-        for row, source, target_row, half in relays:
-            start = starts[0] if source == nx - 1 else starts[1]
-
-            @pl.when(r == row)
-            def _(target_row=target_row, half=half, start=start):
-                copy = forward_copy(turn, half, i, dst, start, target_row)
-                if begin:
-                    hop_copy(turn, half, i, 0, 0).wait_recv()
-                    copy.start()
-                else:
-                    copy.wait_send()
-
-    def arrivals(turn, dst, starts):
-        for row, source, target_row, half in relays:
-            start = starts[0] if source == nx - 1 else starts[1]
-
-            @pl.when(r == target_row)
-            def _(row=row, half=half, start=start):
-                for i in range(2):
-                    forward_copy(turn, half, i, dst, start, row).wait_recv()
-
     for d in range(4):
         when(halo_has[d], lambda d=d: halo_copy(d).start())
-        if d == 1:
-            hops(0, (0, 4), lambda copy: copy.start())
     for load in loads[3:]:
         load.start()
 
@@ -288,13 +232,11 @@
         messages(xs, g * GROUP)
         put_rows(g2f, g * GROUP, dot(xs, wu[...]))
 
-    forward(0, 0, halo, (0, 4), True)
-
     def write_plan(at, rows):
         for i, row in enumerate(rows):
             plan_v[at + i : at + i + 1, :] = row
 
-    write_plan(0, sort_plan([adj_ref[0, k, t] for t in range(NT) for k in range(K)], per=K))
+    write_plan(0, sort_plan([outer_first(adj_ref[0, k, t], NT, NT) for t in range(NT) for k in range(K)], per=K))
     write_plan(6, sort_plan([dsend_ref[0, d, s] for d in range(2) for s in range(4)])[:4])
     write_plan(10, sort_plan([1 - mask_ref[0, g] for g in range(NT)])[:1])
     write_plan(11, sort_plan([send_ref[0, d, b] for d in range(4) for b in range(4)])[:4])
@@ -303,16 +245,13 @@
     first.wait()
     hidden = [plan[10, s] for s in range(SLOTS)]
     edge_list = [(hidden[s], k) for s in range(SLOTS) for k in range(KD)]
-    write_plan(16, sort_plan([didx_ref[k, 0, g] for g, k in edge_list], [g * KD + k for g, k in edge_list], KD))
+    write_plan(16, sort_plan([outer_first(didx_ref[k, 0, g], NT, 8) for g, k in edge_list], [g * KD + k for g, k in edge_list], KD))
     second = pltpu.make_async_copy(plan_v.at[pl.ds(16, 8)], plan.at[pl.ds(16, 8)], plan_sem.at[1])
     second.start()
     second.wait()
 
-    forward(0, 1, halo, (0, 4), True)
     for d in (3, 2, 0, 1):
         when(from_has[d], lambda d=d: halo_copy(d).wait_recv())
-        if d == 0:
-            arrivals(0, halo, (0, 4))
         messages(rows_of(halo, d * 4), NT + d * 4)
 
     for i in (3, 4, 5):
@@ -337,7 +276,6 @@
 
     for d in range(4):
         when(halo_has[d], lambda d=d: halo_copy(d).wait_send())
-    hops(0, (0, 4), lambda copy: copy.wait_send())
     for d in range(2):
         for s in range(4):
             pref[NE + d * 4 + s] = pref[dsend_ref[0, d, s]]
@@ -393,15 +331,16 @@
     def spread_of(at, tile):
         return plan[at + 3, tile].astype(F32) * pref[plan[at + 2, tile]].astype(F32)
 
-    spread(16, 0, DEC_EDGES, decw, pool4)
+    spread(16, 0, SLOTS * (KD - 1), decw, pool4)
     for e in range(8):
-        pref[48 + e] = spread_of(16, NT + e).astype(BF16)
+        pref[48 + e] = spread_of(16, e).astype(BF16)
     returns = [
         send(pref.at[pl.ds(48, 4)], rgin.at[pl.ds(4, 4)], rg_s.at[0], rg_r.at[0], west),
         send(pref.at[pl.ds(52, 4)], rgin.at[pl.ds(0, 4)], rg_s.at[1], rg_r.at[1], east),
     ]
     for item in returns:
         item.start()
+    spread(16, SLOTS * (KD - 1), DEC_EDGES, decw, pool4)
 
     def job_copy(j, sem, src, dst, device):
         return send(src, dst, job_s.at[j, sem], job_r.at[j, sem], device)
@@ -552,7 +491,7 @@
 
     @pl.loop(0, NT)
     def _(t):
-        value = spread_of(16, t).astype(BF16).astype(F32)
+        value = spread_of(16, 8 + t).astype(BF16).astype(F32)
         value = value + plan[9, t].astype(F32) * pref[40 + plan[8, t]].astype(F32)
         g2f[t] = value
         pool4[t] = value.astype(BF16)
@@ -576,22 +515,24 @@
     gradient(1792, [(agg, 0, NT)], [(pool0, 0)])
     job_stage(3, 0)
     job_stage(2, 1)
-    spread(0, 0, ADJ_EDGES // 2, adjw, pool1)
+    outer_edges = NT * (K - 1)
+    spread(0, 0, outer_edges // 2, adjw, pool1)
     job_stage(0, 3)
     job_stage(3, 1)
     job_stage(1, 2)
-    spread(0, ADJ_EDGES // 2, ADJ_EDGES, adjw, pool1)
+    spread(0, outer_edges // 2, outer_edges, adjw, pool1)
 
     def message_slope(e):
-        mbuf[e] = (spread_of(0, e) * msl[e].astype(F32)).astype(BF16)
+        key = lax.rem(e + NT, NE)
+        mbuf[e] = (spread_of(0, key) * msl[e].astype(F32)).astype(BF16)
 
     back_to = (north, south, west, east)
-    back_has = (to_north, to_south, None, None)
-    back_from = (to_south, to_north, None, None)
+    back_has = (has_north, has_south, None, None)
+    back_from = (has_south, has_north, None, None)
 
     def back_copy(d):
         dst = (backns.at[pl.ds(0, 4)], backns.at[pl.ds(4, 4)], redge.at[pl.ds(0, 4)], redge.at[pl.ds(4, 4)])[d]
-        return send(pool1.at[pl.ds(d * 4, 4)], dst, hg_s.at[d], hg_r.at[d], back_to[d])
+        return send(usl.at[pl.ds(d * 4, 4)], dst, hg_s.at[d], hg_r.at[d], back_to[d])
 
     for d in range(4):
 
@@ -599,13 +540,12 @@
         def _(b, d=d):
             message_slope(NT + d * 4 + b)
 
-        put_rows(pool1, d * 4, dot_nt(rows_of(mbuf, NT + d * 4), wm[...]).astype(BF16))
+        put_rows(usl, d * 4, dot_nt(rows_of(mbuf, NT + d * 4), wm[...]).astype(BF16))
         when(back_has[d], lambda d=d: back_copy(d).start())
-        if d == 1:
-            hops(1, (4, 0), lambda copy: copy.start())
 
     job_stage(0, 4)
     job_stage(2, 2)
+    spread(0, outer_edges, ADJ_EDGES, adjw, pool1)
 
     @pl.loop(0, NT)
     def _(e):
@@ -616,13 +556,11 @@
     left, right = [(nv, 0, NT), (halo, 0, NT)], [(mbuf, 0), (mbuf, NT)]
     gradient(2304, left, right, (0,))
     job_stage(4, 0)
-    forward(1, 0, backns, (4, 0), True)
     job_stage(0, 5)
     job_stage(2, 3)
     gradient(2304, left, right, (1,))
     job_stage(5, 0)
     job_stage(4, 1)
-    forward(1, 1, backns, (4, 0), True)
     job_stage(3, 3)
     job_stage(1, 4)
 
@@ -644,7 +582,6 @@
     job_stage(1, 6)
     for d in range(4):
         when(back_from[d], lambda d=d: back_copy(d).wait_recv())
-    arrivals(1, backns, (4, 0))
     for e in range(8):
         pref[e] = backns[e]
         pref[8 + e] = redge[e]
@@ -674,10 +611,6 @@
     lat_out.wait()
     for d in range(4):
         when(back_has[d], lambda d=d: back_copy(d).wait_send())
-    hops(1, (4, 0), lambda copy: copy.wait_send())
-    for turn in range(2):
-        for i in range(2):
-            forward(turn, i, (halo, backns)[turn], (0, 4), False)
 
 
 def finish(lat_ref, m_ref, u_ref, a_ref, o_ref, d_ref, h_ref,
@@ -712,7 +645,7 @@
         pltpu.VMEM((GRAD_ROWS, HALF), BF16), pltpu.VMEM((GRAD_ROWS, HALF), BF16),
         pltpu.VMEM((n - 1, GRAD_ROWS // n, HALF), BF16), pltpu.VMEM((GRAD_ROWS // n, HALF), BF16),
         pltpu.VMEM((n - 1, GRAD_ROWS // n**2, HALF), BF16), pltpu.VMEM((n, GRAD_ROWS // n**2, HALF), BF16),
-        tiles(4), tiles(8),
+        tiles(8),
         pltpu.VMEM((24, 128), jnp.int32), pltpu.SMEM((24, 128), jnp.int32),
         pltpu.SemaphoreType.DMA((9 + NT,)), pltpu.SemaphoreType.DMA((2,)), pltpu.SemaphoreType.DMA((1,)),
         *[pltpu.SemaphoreType.DMA((4,))] * 2,
@@ -720,8 +653,6 @@
         *[pltpu.SemaphoreType.DMA((4,))] * 2,
         *[pltpu.SemaphoreType.DMA((len(JOBS), JOB_SEMS))] * 2,
         pltpu.SemaphoreType.DMA((len(JOBS),)),
-        pltpu.SemaphoreType.DMA((2, 4)), pltpu.SemaphoreType.DMA((2, 2)),
-        pltpu.SemaphoreType.DMA((2, 2)), pltpu.SemaphoreType.DMA((2, 4)),
     ]
     lat, grads = pl.pallas_call(
         functools.partial(kernel, sizes),

time: 136 us -> 129 us (0.949)
  Pallas kernels: 135 us -> 128 us
    pallas_call x1, Pallas kernels: 127 us -> 120 us  [on_device(): pl.pallas_call(functools.partial(kernel, sizes), out_shape=(jax.ShapeDtyp...]
where the time goes in v2:
time: 129 us
  Pallas kernels  128 us (99%)
    pallas_call x1, Pallas kernels, on_device(): pl.pallas_call(functools.partial(kernel, sizes), out_shape=(jax.ShapeDtyp...  120 us
    pallas_call x1, Pallas kernels, on_device(): pl.pallas_call(finish, out_shape=(f32(NT, TILE, D), *[f32(D, D)] * 5, f32...  7.56 us

profile of v2, /device:TPU:1, one launch (start us, length us, event | category | flops | bytes accessed | tf_op | source)
XLA Modules:
  0.0 128.8 jit_solution(3959762968225149037)
XLA Ops:
  0.6 120.5 %mesh_step.1 = (bf16[16,128,512]{2,1,0:T(8,128)(2,1)}, bf16[2,2816,256]{2,1,0:T(8,128)(2,1)}) custom-call(s32[1,4,4]{2,1,0:T(4,128)} %send_ref.1, s32[1,4,16]{2,1,0:T(4,128)} %bitcast.14, s32[1,2,4]{2,1,0:T(2,128)} %dsend_ref.1, s32[3,1,16]{2,1,0:T(1,128)} %bitcast.15, s32[1,16]{1,0:T(1,128)} %mask_ref.1, bf16[16,128,512]{2,1,0:T(8,128)(2,1)} %bitcast.9, ...), custom_call_target="tpu_custom_call" | custom-call | tf_op jit(solution)/shard_map/mesh_step/pallas_call | solution.py:657
  121.1 7.6 %finish.1 = (f32[16,128,512]{2,1,0:T(8,128)}, f32[512,512]{1,0:T(8,128)}, f32[512,512]{1,0:T(8,128)}, f32[512,512]{1,0:T(8,128)}, f32[512,512]{1,0:T(8,128)}, /*index=5*/f32[512,512]{1,0:T(8,128)}, f32[227,512]{1,0:T(8,128)}) custom-call(bf16[16,128,512]{2,1,0:T(8,128)(2,1)} %get-tuple-element.16.lat_ref, ...), custom_call_target="tpu_custom_call" | custom-call | tf_op jit(solution)/shard_map/finish/pallas_call | solution.py:687

commit v3 on v2

--- a/solution.py
+++ b/solution.py
@@ -28,12 +28,11 @@
 
 JOBS = (
     (0, 768, ("z", "y", "x")),
-    (768, 512, ("y", "x", "z")),
-    (1280, 512, ("x", "z", "y")),
-    (1792, 512, ("z", "x", "y")),
-    (2304, 256, ("y", "z", "x")),
-    (2560, 256, ("z", "y", "x")),
+    (768, 512, ("z", "x", "y")),
+    (1280, 512, ("x", "y", "z")),
+    (1792, 512, ("y", "z", "x")),
 )
+LAST, LAST_ROWS = 2304, 512
 GRAD_ROWS = 2816
 GRAD_F32 = 2304
 HALF = D // 2
@@ -112,9 +111,9 @@
     lat_hbm, grads_hbm,
     nv, halo, adjw, decw, target, wm, wu, wa, wo, wd, wh,
     pref, msl, g2f, agg, hid, usl, redge, rgin, err, pool0, pool1, mbuf, pool4, acc,
-    gbuf, cs, cr, r1, s2, r2, x4,
+    gbuf, cs, cr, r1, s2, r2, x4, rl,
     backns, plan_v, plan,
-    in_sems, plan_sem, out_sem, halo_s, halo_r, edge_s, edge_r, rg_s, rg_r, hg_s, hg_r, job_s, job_r, job_l,
+    in_sems, plan_sem, out_sem, halo_s, halo_r, edge_s, edge_r, rg_s, rg_r, hg_s, hg_r, job_s, job_r, job_l, last_s, last_r,
 ):
     nrow, ncol, nx, ny, nzl = sizes["rows"], sizes["cols"], sizes["x"], sizes["y"], sizes["zl"]
     nzh, n = sizes["zh"], sizes["n"]
@@ -134,6 +133,10 @@
         if axis == "y":
             return (r, (zl * ny + there) * CORES + core), there
         return (lax.div(there, nzl) * nx + x, (lax.rem(there, nzl) * ny + y) * CORES + core), there
+
+    def plane_peer(step):
+        there = lax.rem(x * n + y + step, n * n)
+        return (zh * nx + lax.div(there, n), (zl * ny + lax.rem(there, n)) * CORES + core), there
 
     mate = (r, c + 1 - 2 * core)
     west = (r, lax.rem(c + ncol - 1, ncol))
@@ -161,13 +164,13 @@
     def greet(device):
         pl.semaphore_signal(barrier, inc=1, device_id=device, device_id_type=MESH)
 
-    greeted = 2
     greet(west)
     greet(east)
-    for axis in ("x", "y", "z"):
-        for step in range(1, n):
-            greet(peer(axis, step)[0])
-            greeted += 1
+    for step in range(1, n):
+        greet(peer("z", step)[0])
+    for step in range(1, n * n):
+        greet(plane_peer(step)[0])
+    greeted = 2 + (n - 1) + (n * n - 1)
 
     @pl.when(has_north)
     def _():
@@ -465,6 +468,78 @@
             for item in back_core(j):
                 item.wait()
 
+    chunk = LAST_ROWS // (n * n)
+    last_mine = pl.ds(pl.multiple_of(LAST + (x * n + y) * chunk, 16), chunk)
+    last_place = pl.ds(LAST // (n * n), chunk)
+
+    def last_copy(sem, src, dst, device):
+        return send(src, dst, last_s.at[sem], last_r.at[sem], device)
+
+    def last_core():
+        return last_copy(0, cs.at[pl.ds(LAST, LAST_ROWS)], cr.at[pl.ds(LAST, LAST_ROWS)], mate)
+
+    def last_scatter():
+        out = []
+        for step in range(1, n * n):
+            device, there = plane_peer(step)
+            src = cs.at[pl.ds(pl.multiple_of(LAST + there * chunk, 16), chunk)]
+            out.append(last_copy(step, src, rl.at[step - 1], device))
+        return out
+
+    def last_exchange():
+        mine = x4.at[z, last_place]
+        return [last_copy(n * n + step, mine, mine, peer("z", step)[0]) for step in range(1, n)]
+
+    def last_gather():
+        part = cr.at[last_mine]
+        return [last_copy(n * n + n + step, part, part, plane_peer(step)[0]) for step in range(1, n * n)]
+
+    def last_back():
+        part = pl.ds(LAST, LAST_ROWS)
+        return (
+            last_copy(n * n, cr.at[part], grads_hbm.at[core, part], mate),
+            pltpu.make_async_copy(cr.at[part], grads_hbm.at[core, part], job_l.at[len(JOBS)]),
+        )
+
+    def last_stage(stage_number):
+        whole = pl.ds(LAST, LAST_ROWS)
+        if stage_number == 0:
+            low, high = gbuf[:LAST_ROWS, :HALF], gbuf[:LAST_ROWS, HALF:]
+            cs[whole] = jnp.where(core == 0, high, low).astype(BF16)
+            last_core().start()
+        elif stage_number == 1:
+            last_core().wait()
+            low, high = gbuf[:LAST_ROWS, :HALF], gbuf[:LAST_ROWS, HALF:]
+            cs[whole] = (jnp.where(core == 0, low, high) + cr[whole].astype(F32)).astype(BF16)
+            for item in last_scatter():
+                item.start()
+        elif stage_number == 2:
+            for item in last_scatter():
+                item.wait()
+            total = cs[last_mine].astype(F32)
+            for step in range(n * n - 1):
+                total = total + rl[step].astype(F32)
+            x4[z, last_place] = total.astype(BF16)
+            for item in last_exchange():
+                item.start()
+        elif stage_number == 3:
+            for item in last_exchange():
+                item.wait()
+            total = x4[0, last_place].astype(F32)
+            for other in range(1, n):
+                total = total + x4[other, last_place].astype(F32)
+            cr[last_mine] = (total * (1.0 / (nrow * ncol))).astype(BF16)
+            for item in last_gather():
+                item.start()
+        elif stage_number == 4:
+            for item in last_gather():
+                item.wait()
+            for item in last_back():
+                item.start()
+        else:
+            for item in last_back():
+                item.wait()
+
     def gradient(at, left, right, halves=(0, 1)):
         for half in halves:
             lanes = slice(half * HALF, (half + 1) * HALF)
@@ -508,18 +583,16 @@
         put_rows(g2f, g * GROUP, rows_of(g2f, g * GROUP) + dot_nt(slope, wu[...]))
         put_rows(pool1, g * GROUP, dot_nt(slope, wa[...]).astype(BF16))
 
-    job_stage(0, 2)
-    job_stage(1, 1)
     gradient(1280, [(nv, 0, NT)], [(pool0, 0)])
     job_stage(2, 0)
+    job_stage(1, 1)
     gradient(1792, [(agg, 0, NT)], [(pool0, 0)])
     job_stage(3, 0)
-    job_stage(2, 1)
+    job_stage(0, 2)
     outer_edges = NT * (K - 1)
     spread(0, 0, outer_edges // 2, adjw, pool1)
-    job_stage(0, 3)
+    job_stage(2, 1)
     job_stage(3, 1)
-    job_stage(1, 2)
     spread(0, outer_edges // 2, outer_edges, adjw, pool1)
 
     def message_slope(e):
@@ -543,50 +616,48 @@
         put_rows(usl, d * 4, dot_nt(rows_of(mbuf, NT + d * 4), wm[...]).astype(BF16))
         when(back_has[d], lambda d=d: back_copy(d).start())
 
-    job_stage(0, 4)
-    job_stage(2, 2)
     spread(0, outer_edges, ADJ_EDGES, adjw, pool1)
 
     @pl.loop(0, NT)
     def _(e):
         message_slope(e)
 
-    job_stage(1, 3)
+    left, right = [(nv, 0, NT), (halo, 0, NT)], [(mbuf, 0), (mbuf, NT)]
+    gradient(LAST, left, right)
+    last_stage(0)
+    job_stage(0, 3)
+    job_stage(1, 2)
+    last_stage(1)
+    job_stage(2, 2)
     job_stage(3, 2)
-    left, right = [(nv, 0, NT), (halo, 0, NT)], [(mbuf, 0), (mbuf, NT)]
-    gradient(2304, left, right, (0,))
-    job_stage(4, 0)
-    job_stage(0, 5)
-    job_stage(2, 3)
-    gradient(2304, left, right, (1,))
-    job_stage(5, 0)
-    job_stage(4, 1)
-    job_stage(3, 3)
-    job_stage(1, 4)
 
     @pl.loop(0, NT // GROUP)
     def _(g):
         put_rows(g2f, g * GROUP, rows_of(g2f, g * GROUP) + dot_nt(rows_of(mbuf, g * GROUP), wm[...]))
 
-    job_stage(5, 1)
-    job_stage(0, 6)
+    job_stage(1, 3)
+    job_stage(0, 4)
+    last_stage(2)
+    job_stage(2, 3)
+    job_stage(3, 3)
+    job_stage(1, 4)
+    job_stage(0, 5)
+    last_stage(3)
     job_stage(2, 4)
-    job_stage(4, 2)
     job_stage(3, 4)
     job_stage(1, 5)
-    job_stage(5, 2)
+    job_stage(0, 6)
     job_stage(2, 5)
-    job_stage(4, 3)
     job_stage(3, 5)
-    job_stage(5, 3)
     job_stage(1, 6)
+    last_stage(4)
+    job_stage(2, 6)
+    job_stage(3, 6)
     for d in range(4):
         when(back_from[d], lambda d=d: back_copy(d).wait_recv())
     for e in range(8):
         pref[e] = backns[e]
         pref[8 + e] = redge[e]
-    job_stage(4, 4)
-    job_stage(5, 4)
     total = None
     for p in range(16):
         arrived = pref[plan[11, p]].astype(F32)
@@ -600,27 +671,49 @@
 
     lat_out = pltpu.make_async_copy(agg, lat_hbm, out_sem.at[0])
     lat_out.start()
-    for stage in range(5, 7):
-        for j in (4, 5):
-            job_stage(j, stage)
-        if stage == 5:
-            job_stage(2, 6)
-            job_stage(3, 6)
     for j in range(len(JOBS)):
         job_stage(j, 7)
+    last_stage(5)
     lat_out.wait()
     for d in range(4):
         when(back_has[d], lambda d=d: back_copy(d).wait_send())
 
 
-def finish(lat_ref, m_ref, u_ref, a_ref, o_ref, d_ref, h_ref,
-           latent_ref, msg_ref, upd_ref, agg_ref, out_ref, dec_ref, head_ref):
-    latent_ref[...] = lat_ref[...].astype(F32)
-    for src, dst in (
-        (m_ref, msg_ref), (u_ref, upd_ref), (a_ref, agg_ref), (o_ref, out_ref), (d_ref, dec_ref), (h_ref, head_ref),
-    ):
-        dst[:, :HALF] = src[0].astype(F32)
-        dst[:, HALF:] = src[1].astype(F32)
+SQUARES = (2304, 1280, 1792, 768, 0)
+LAT_PARTS = 4
+
+
+def finish(lat_hbm, grads_hbm, latent_hbm, msg_hbm, upd_hbm, agg_hbm, out_hbm, dec_hbm, head_hbm,
+           lat, grads, latent, squares, head, in_sems, out_sems):
+    per = NT // LAT_PARTS
+    parts = [pl.ds(i * per, per) for i in range(LAT_PARTS)]
+    loads = [pltpu.make_async_copy(lat_hbm.at[part], lat.at[part], in_sems.at[i]) for i, part in enumerate(parts)]
+    for i, (at, rows) in enumerate([(at, D) for at in SQUARES] + [(D, HALF)]):
+        part = pl.ds(at, rows)
+        loads.append(pltpu.make_async_copy(grads_hbm.at[:, part], grads.at[:, part], in_sems.at[LAT_PARTS + i]))
+    for load in loads:
+        load.start()
+    stores = []
+
+    def store(src, dst):
+        stores.append(pltpu.make_async_copy(src, dst, out_sems.at[len(stores)]))
+        stores[-1].start()
+
+    for i, part in enumerate(parts):
+        loads[i].wait()
+        latent[part] = lat[part].astype(F32)
+        store(latent.at[part], latent_hbm.at[part])
+    for i, (at, dst) in enumerate(zip(SQUARES, (msg_hbm, upd_hbm, agg_hbm, out_hbm, dec_hbm))):
+        loads[LAT_PARTS + i].wait()
+        for half in range(2):
+            squares[i, :, half * HALF : (half + 1) * HALF] = grads[half, at : at + D].astype(F32)
+        store(squares.at[i], dst)
+    loads[-1].wait()
+    for half in range(2):
+        head[:, half * HALF : (half + 1) * HALF] = grads[half, D : D + HALF].astype(F32)[:OUTC]
+    store(head, head_hbm)
+    for item in stores:
+        item.wait()
 
 
 def on_device(
@@ -643,8 +736,9 @@
         pltpu.VMEM((TILE, D), F32),
         pltpu.VMEM((GRAD_F32, D), F32),
         pltpu.VMEM((GRAD_ROWS, HALF), BF16), pltpu.VMEM((GRAD_ROWS, HALF), BF16),
-        pltpu.VMEM((n - 1, GRAD_ROWS // n, HALF), BF16), pltpu.VMEM((GRAD_ROWS // n, HALF), BF16),
-        pltpu.VMEM((n - 1, GRAD_ROWS // n**2, HALF), BF16), pltpu.VMEM((n, GRAD_ROWS // n**2, HALF), BF16),
+        pltpu.VMEM((n - 1, LAST // n, HALF), BF16), pltpu.VMEM((LAST // n, HALF), BF16),
+        pltpu.VMEM((n - 1, LAST // n**2, HALF), BF16), pltpu.VMEM((n, GRAD_ROWS // n**2, HALF), BF16),
+        pltpu.VMEM((n * n - 1, LAST_ROWS // n**2, HALF), BF16),
         tiles(8),
         pltpu.VMEM((24, 128), jnp.int32), pltpu.SMEM((24, 128), jnp.int32),
         pltpu.SemaphoreType.DMA((9 + NT,)), pltpu.SemaphoreType.DMA((2,)), pltpu.SemaphoreType.DMA((1,)),
@@ -652,7 +746,8 @@
         *[pltpu.SemaphoreType.DMA((2,))] * 4,
         *[pltpu.SemaphoreType.DMA((4,))] * 2,
         *[pltpu.SemaphoreType.DMA((len(JOBS), JOB_SEMS))] * 2,
-        pltpu.SemaphoreType.DMA((len(JOBS),)),
+        pltpu.SemaphoreType.DMA((len(JOBS) + 1,)),
+        *[pltpu.SemaphoreType.DMA((2 * n * n + n,))] * 2,
     ]
     lat, grads = pl.pallas_call(
         functools.partial(kernel, sizes),
@@ -675,24 +770,20 @@
         target.T,
         w_msg, w_update, w_aggregate, w_output, w_decode, w_head.T,
     )
-    steps = 8
-    block = D // steps
-
-    def rows_spec(at, size=block):
-        return pl.BlockSpec((CORES, size, HALF), lambda i: (0, at // size + i, 0))
-
-    latents = pl.BlockSpec((NT // steps, TILE, D), lambda i: (i, 0, 0))
-    square = pl.BlockSpec((block, D), lambda i: (i, 0))
     f32 = lambda *shape: jax.ShapeDtypeStruct(shape, F32)
     outs = pl.pallas_call(
         finish,
         out_shape=(f32(NT, TILE, D), *[f32(D, D)] * 5, f32(OUTC, D)),
-        grid=(steps,),
-        in_specs=[latents, *(rows_spec(at) for at in (2304, 1280, 1792, 768, 0)), rows_spec(512, HALF // steps)],
-        out_specs=(latents, *[square] * 5, pl.BlockSpec((HALF // steps, D), lambda i: (i, 0))),
+        in_specs=[any_spec] * 2,
+        out_specs=(any_spec,) * 7,
+        scratch_shapes=[
+            tiles(NT), pltpu.VMEM((CORES, GRAD_ROWS, HALF), BF16),
+            tiles(NT, F32), pltpu.VMEM((5, D, D), F32), pltpu.VMEM((OUTC, D), F32),
+            pltpu.SemaphoreType.DMA((LAT_PARTS + 6,)), pltpu.SemaphoreType.DMA((LAT_PARTS + 6,)),
+        ],
         compiler_params=pltpu.CompilerParams(vmem_limit_bytes=60 * 1024 * 1024),
         name="finish",
-    )(lat, grads, grads, grads, grads, grads, grads)
+    )(lat, grads)
     latent, msg, upd, agg, out, dec, head = outs
     return latent.reshape(NT * TILE, D), msg, upd, agg, out, dec, head.T
 

time: 129 us -> 122 us (0.946)
  Pallas kernels: 128 us -> 121 us
    pallas_call x1, Pallas kernels: 120 us -> 116 us  [on_device(): pl.pallas_call(functools.partial(kernel, sizes), out_shape=(jax.ShapeDtyp...]
    pallas_call x1, Pallas kernels: 7.56 us -> 5.02 us  [on_device(): pl.pallas_call(finish, out_shape=(f32(NT, TILE, D), *[f32(D, D)] * 5, f32...]
where the time goes in v3:
time: 122 us
  Pallas kernels  121 us (99%)
    pallas_call x1, Pallas kernels, on_device(): pl.pallas_call(functools.partial(kernel, sizes), out_shape=(jax.ShapeDtyp...  116 us
    pallas_call x1, Pallas kernels, on_device(): pl.pallas_call(finish, out_shape=(f32(NT, TILE, D), *[f32(D, D)] * 5, f32...  5.02 us

profile of v3, /device:TPU:1, one launch (start us, length us, event | category | flops | bytes accessed | tf_op | source)
XLA Modules:
  0.0 121.5 jit_solution(10918006104376171839)
XLA Ops:
  0.6 115.7 %mesh_step.1 = (bf16[16,128,512]{2,1,0:T(8,128)(2,1)}, bf16[2,2816,256]{2,1,0:T(8,128)(2,1)}) custom-call(s32[1,4,4]{2,1,0:T(4,128)} %send_ref.1, s32[1,4,16]{2,1,0:T(4,128)} %bitcast.14, s32[1,2,4]{2,1,0:T(2,128)} %dsend_ref.1, s32[3,1,16]{2,1,0:T(1,128)} %bitcast.15, s32[1,16]{1,0:T(1,128)} %mask_ref.1, bf16[16,128,512]{2,1,0:T(8,128)(2,1)} %bitcast.9, ...), custom_call_target="tpu_custom_call" | custom-call | tf_op jit(solution)/shard_map/mesh_step/pallas_call | solution.py:752
  116.3 5.0 %finish.1 = (f32[16,128,512]{2,1,0:T(8,128)}, f32[512,512]{1,0:T(8,128)}, f32[512,512]{1,0:T(8,128)}, f32[512,512]{1,0:T(8,128)}, f32[512,512]{1,0:T(8,128)}, /*index=5*/f32[512,512]{1,0:T(8,128)}, f32[227,512]{1,0:T(8,128)}) custom-call(bf16[16,128,512]{2,1,0:T(8,128)(2,1)} %get-tuple-element.16.lat_hbm, bf16[2,2816,256]{2,1,0:T(8,128)(2,1)} %get-tuple-element.17.grads_hbm), custom_call_target="tpu_custom_call" | custom-call | tf_op jit(solution)/shard_map/finish/pallas_call | solution.py:774

commit v4 on v3

--- a/solution.py
+++ b/solution.py
@@ -27,16 +27,13 @@
 CORES = 2
 
 JOBS = (
-    (0, 768, ("z", "y", "x")),
-    (768, 512, ("z", "x", "y")),
-    (1280, 512, ("x", "y", "z")),
-    (1792, 512, ("y", "z", "x")),
+    (0, 768, ("x", "y"), "z"),
+    (768, 1536, ("y", "z"), "x"),
+    (2304, 512, ("x", "y"), "z"),
 )
-LAST, LAST_ROWS = 2304, 512
 GRAD_ROWS = 2816
 GRAD_F32 = 2304
 HALF = D // 2
-JOB_SEMS = 17
 
 
 def axes_of(rows, cols):
@@ -111,9 +108,9 @@
     lat_hbm, grads_hbm,
     nv, halo, adjw, decw, target, wm, wu, wa, wo, wd, wh,
     pref, msl, g2f, agg, hid, usl, redge, rgin, err, pool0, pool1, mbuf, pool4, acc,
-    gbuf, cs, cr, r1, s2, r2, x4, rl,
+    gbuf, cs, cr, r1, x4,
     backns, plan_v, plan,
-    in_sems, plan_sem, out_sem, halo_s, halo_r, edge_s, edge_r, rg_s, rg_r, hg_s, hg_r, job_s, job_r, job_l, last_s, last_r,
+    in_sems, plan_sem, out_sem, halo_s, halo_r, edge_s, edge_r, rg_s, rg_r, hg_s, hg_r, job_s, job_r, job_l,
 ):
     nrow, ncol, nx, ny, nzl = sizes["rows"], sizes["cols"], sizes["x"], sizes["y"], sizes["zl"]
     nzh, n = sizes["zh"], sizes["n"]
@@ -126,17 +123,18 @@
     z = zh * nzl + zl
     place = {"x": x, "y": y, "z": z}
 
-    def peer(axis, step):
-        there = lax.rem(place[axis] + step, n)
-        if axis == "x":
-            return (zh * nx + there, c), there
-        if axis == "y":
-            return (r, (zl * ny + there) * CORES + core), there
-        return (lax.div(there, nzl) * nx + x, (lax.rem(there, nzl) * ny + y) * CORES + core), there
-
-    def plane_peer(step):
-        there = lax.rem(x * n + y + step, n * n)
-        return (zh * nx + lax.div(there, n), (zl * ny + lax.rem(there, n)) * CORES + core), there
+    def device_at(**moved):
+        at = {**place, **moved}
+        zhi, zlo = lax.div(at["z"], nzl), lax.rem(at["z"], nzl)
+        return (zhi * nx + at["x"], (zlo * ny + at["y"]) * CORES + core)
+
+    def line_peer(axis, step):
+        return device_at(**{axis: lax.rem(place[axis] + step, n)})
+
+    def plane_peer(axes, step):
+        a, b = axes
+        there = lax.rem(place[a] * n + place[b] + step, n * n)
+        return device_at(**{a: lax.div(there, n), b: lax.rem(there, n)}), there
 
     mate = (r, c + 1 - 2 * core)
     west = (r, lax.rem(c + ncol - 1, ncol))
@@ -166,11 +164,11 @@
 
     greet(west)
     greet(east)
-    for step in range(1, n):
-        greet(peer("z", step)[0])
-    for step in range(1, n * n):
-        greet(plane_peer(step)[0])
-    greeted = 2 + (n - 1) + (n * n - 1)
+    planes = (("x", "y"), ("y", "z"))
+    for axes in planes:
+        for step in range(1, n * n):
+            greet(plane_peer(axes, step)[0])
+    greeted = 2 + len(planes) * (n * n - 1)
 
     @pl.when(has_north)
     def _():
@@ -348,196 +346,83 @@
     def job_copy(j, sem, src, dst, device):
         return send(src, dst, job_s.at[j, sem], job_r.at[j, sem], device)
 
-    def c_copy(j):
-        at, rows, _ = JOBS[j]
+    def core_out(j):
+        at, rows = JOBS[j][:2]
         return job_copy(j, 0, cs.at[pl.ds(at, rows)], cr.at[pl.ds(at, rows)], mate)
 
-    def first_copies(j):
-        at, rows, order = JOBS[j]
-        quarter = rows // n
+    def scatter(j):
+        at, rows, axes, _ = JOBS[j]
+        chunk = rows // (n * n)
         out = []
-        for step in range(1, n):
-            device, there = peer(order[0], step)
-            src = cs.at[pl.ds(pl.multiple_of(at + there * quarter, 16), quarter)]
-            out.append(job_copy(j, step, src, r1.at[step - 1, pl.ds(at // n, quarter)], device))
+        for step in range(1, n * n):
+            device, there = plane_peer(axes, step)
+            src = cs.at[pl.ds(pl.multiple_of(at + there * chunk, 16), chunk)]
+            out.append(job_copy(j, step, src, r1.at[step - 1, pl.ds(at // (n * n), chunk)], device))
         return out
 
-    def second_copies(j):
-        at, rows, order = JOBS[j]
-        small = rows // (n * n)
-        out = []
-        for step in range(1, n):
-            device, there = peer(order[1], step)
-            src = s2.at[pl.ds(pl.multiple_of(at // n + there * small, 16), small)]
-            out.append(job_copy(j, 3 + step, src, r2.at[step - 1, pl.ds(at // (n * n), small)], device))
-        return out
-
-    def third_copies(j):
-        at, rows, order = JOBS[j]
-        small = rows // (n * n)
-        out = []
-        for step in range(1, n):
-            device, _ = peer(order[2], step)
-            mine = x4.at[place[order[2]], pl.ds(at // (n * n), small)]
-            out.append(job_copy(j, 6 + step, mine, mine, device))
-        return out
-
-    def small_at(j):
-        at, rows, order = JOBS[j]
-        quarter, small = rows // n, rows // (n * n)
-        return pl.multiple_of(at + place[order[0]] * quarter + place[order[1]] * small, 16)
-
-    def back_small(j):
-        at, rows, order = JOBS[j]
-        part = cr.at[pl.ds(small_at(j), rows // (n * n))]
+    def exchange(j):
+        at, rows, _, axis = JOBS[j]
+        mine = x4.at[place[axis], pl.ds(at // (n * n), rows // (n * n))]
+        return [job_copy(j, n * n + step, mine, mine, line_peer(axis, step)) for step in range(1, n)]
+
+    def own_chunk(j):
+        at, rows, (a, b), _ = JOBS[j]
+        chunk = rows // (n * n)
+        return pl.ds(pl.multiple_of(at + (place[a] * n + place[b]) * chunk, 16), chunk)
+
+    def gather(j):
+        part = cr.at[own_chunk(j)]
         return [
-            job_copy(j, 9 + step, part, part, peer(order[1], step)[0]) for step in range(1, n)
+            job_copy(j, n * n + n + step, part, part, plane_peer(JOBS[j][2], step)[0]) for step in range(1, n * n)
         ]
 
-    def back_quarter(j):
-        at, rows, order = JOBS[j]
-        quarter = rows // n
-        part = cr.at[pl.ds(pl.multiple_of(at + place[order[0]] * quarter, 16), quarter)]
-        return [
-            job_copy(j, 12 + step, part, part, peer(order[0], step)[0]) for step in range(1, n)
-        ]
-
-    def back_core(j):
-        at, rows, _ = JOBS[j]
+    def core_back(j):
+        at, rows = JOBS[j][:2]
         part = pl.ds(at, rows)
         return (
-            job_copy(j, 16, cr.at[part], grads_hbm.at[core, part], mate),
+            job_copy(j, n * n, cr.at[part], grads_hbm.at[core, part], mate),
             pltpu.make_async_copy(cr.at[part], grads_hbm.at[core, part], job_l.at[j]),
         )
 
     def job_stage(j, stage_number):
-        at, rows, order = JOBS[j]
-        quarter, small = rows // n, rows // (n * n)
-        whole = pl.ds(at, rows)
-        own = pl.ds(at % GRAD_F32, rows)
+        at, rows, _, axis = JOBS[j]
+        whole, own = pl.ds(at, rows), pl.ds(at % GRAD_F32, rows)
+        small = pl.ds(at // (n * n), rows // (n * n))
         if stage_number == 0:
             low, high = gbuf[own, :HALF], gbuf[own, HALF:]
             cs[whole] = jnp.where(core == 0, high, low).astype(BF16)
-            c_copy(j).start()
+            core_out(j).start()
         elif stage_number == 1:
-            c_copy(j).wait()
+            core_out(j).wait()
             low, high = gbuf[own, :HALF], gbuf[own, HALF:]
             cs[whole] = (jnp.where(core == 0, low, high) + cr[whole].astype(F32)).astype(BF16)
-            for item in first_copies(j):
+            for item in scatter(j):
                 item.start()
         elif stage_number == 2:
-            mine = pl.ds(pl.multiple_of(at + place[order[0]] * quarter, 16), quarter)
-            for item in first_copies(j):
+            for item in scatter(j):
                 item.wait()
-            total = cs[mine].astype(F32)
-            for step in range(n - 1):
-                total = total + r1[step, pl.ds(at // n, quarter)].astype(F32)
-            s2[pl.ds(at // n, quarter)] = total.astype(BF16)
-            for item in second_copies(j):
+            total = cs[own_chunk(j)].astype(F32)
+            for step in range(n * n - 1):
+                total = total + r1[step, small].astype(F32)
+            x4[place[axis], small] = total.astype(BF16)
+            for item in exchange(j):
                 item.start()
         elif stage_number == 3:
-            mine = pl.ds(pl.multiple_of(at // n + place[order[1]] * small, 16), small)
-            for item in second_copies(j):
+            for item in exchange(j):
                 item.wait()
-            total = s2[mine].astype(F32)
-            for step in range(n - 1):
-                total = total + r2[step, pl.ds(at // (n * n), small)].astype(F32)
-            x4[place[order[2]], pl.ds(at // (n * n), small)] = total.astype(BF16)
-            for item in third_copies(j):
+            total = x4[0, small].astype(F32)
+            for other in range(1, n):
+                total = total + x4[other, small].astype(F32)
+            cr[own_chunk(j)] = (total * (1.0 / (nrow * ncol))).astype(BF16)
+            for item in gather(j):
                 item.start()
         elif stage_number == 4:
-            for item in third_copies(j):
+            for item in gather(j):
                 item.wait()
-            total = x4[0, pl.ds(at // (n * n), small)].astype(F32)
-            for other in range(1, n):
-                total = total + x4[other, pl.ds(at // (n * n), small)].astype(F32)
-            cr[pl.ds(small_at(j), small)] = (total * (1.0 / (nrow * ncol))).astype(BF16)
-            for item in back_small(j):
-                item.start()
-        elif stage_number == 5:
-            for item in back_small(j):
-                item.wait()
-            for item in back_quarter(j):
-                item.start()
-        elif stage_number == 6:
-            for item in back_quarter(j):
-                item.wait()
-            for item in back_core(j):
+            for item in core_back(j):
                 item.start()
         else:
-            for item in back_core(j):
-                item.wait()
-
-    chunk = LAST_ROWS // (n * n)
-    last_mine = pl.ds(pl.multiple_of(LAST + (x * n + y) * chunk, 16), chunk)
-    last_place = pl.ds(LAST // (n * n), chunk)
-
-    def last_copy(sem, src, dst, device):
-        return send(src, dst, last_s.at[sem], last_r.at[sem], device)
-
-    def last_core():
-        return last_copy(0, cs.at[pl.ds(LAST, LAST_ROWS)], cr.at[pl.ds(LAST, LAST_ROWS)], mate)
-
-    def last_scatter():
-        out = []
-        for step in range(1, n * n):
-            device, there = plane_peer(step)
-            src = cs.at[pl.ds(pl.multiple_of(LAST + there * chunk, 16), chunk)]
-            out.append(last_copy(step, src, rl.at[step - 1], device))
-        return out
-
-    def last_exchange():
-        mine = x4.at[z, last_place]
-        return [last_copy(n * n + step, mine, mine, peer("z", step)[0]) for step in range(1, n)]
-
-    def last_gather():
-        part = cr.at[last_mine]
-        return [last_copy(n * n + n + step, part, part, plane_peer(step)[0]) for step in range(1, n * n)]
-
-    def last_back():
-        part = pl.ds(LAST, LAST_ROWS)
-        return (
-            last_copy(n * n, cr.at[part], grads_hbm.at[core, part], mate),
-            pltpu.make_async_copy(cr.at[part], grads_hbm.at[core, part], job_l.at[len(JOBS)]),
-        )
-
-    def last_stage(stage_number):
-        whole = pl.ds(LAST, LAST_ROWS)
-        if stage_number == 0:
-            low, high = gbuf[:LAST_ROWS, :HALF], gbuf[:LAST_ROWS, HALF:]
-            cs[whole] = jnp.where(core == 0, high, low).astype(BF16)
-            last_core().start()
-        elif stage_number == 1:
-            last_core().wait()
-            low, high = gbuf[:LAST_ROWS, :HALF], gbuf[:LAST_ROWS, HALF:]
-            cs[whole] = (jnp.where(core == 0, low, high) + cr[whole].astype(F32)).astype(BF16)
-            for item in last_scatter():
-                item.start()
-        elif stage_number == 2:
-            for item in last_scatter():
-                item.wait()
-            total = cs[last_mine].astype(F32)
-            for step in range(n * n - 1):
-                total = total + rl[step].astype(F32)
-            x4[z, last_place] = total.astype(BF16)
-            for item in last_exchange():
-                item.start()
-        elif stage_number == 3:
-            for item in last_exchange():
-                item.wait()
-            total = x4[0, last_place].astype(F32)
-            for other in range(1, n):
-                total = total + x4[other, last_place].astype(F32)
-            cr[last_mine] = (total * (1.0 / (nrow * ncol))).astype(BF16)
-            for item in last_gather():
-                item.start()
-        elif stage_number == 4:
-            for item in last_gather():
-                item.wait()
-            for item in last_back():
-                item.start()
-        else:
-            for item in last_back():
+            for item in core_back(j):
                 item.wait()
 
     def gradient(at, left, right, halves=(0, 1)):
@@ -573,7 +458,6 @@
 
     job_stage(0, 1)
     gradient(768, [(hid, 0, NT)], [(pool4, 0)])
-    job_stage(1, 0)
 
     @pl.loop(0, NT // GROUP)
     def _(g):
@@ -584,15 +468,13 @@
         put_rows(pool1, g * GROUP, dot_nt(slope, wa[...]).astype(BF16))
 
     gradient(1280, [(nv, 0, NT)], [(pool0, 0)])
-    job_stage(2, 0)
-    job_stage(1, 1)
     gradient(1792, [(agg, 0, NT)], [(pool0, 0)])
-    job_stage(3, 0)
+    job_stage(1, 0)
     job_stage(0, 2)
     outer_edges = NT * (K - 1)
     spread(0, 0, outer_edges // 2, adjw, pool1)
-    job_stage(2, 1)
-    job_stage(3, 1)
+    job_stage(1, 1)
+    job_stage(0, 3)
     spread(0, outer_edges // 2, outer_edges, adjw, pool1)
 
     def message_slope(e):
@@ -623,36 +505,19 @@
         message_slope(e)
 
     left, right = [(nv, 0, NT), (halo, 0, NT)], [(mbuf, 0), (mbuf, NT)]
-    gradient(LAST, left, right)
-    last_stage(0)
-    job_stage(0, 3)
+    gradient(2304, left, right)
+    job_stage(2, 0)
     job_stage(1, 2)
-    last_stage(1)
-    job_stage(2, 2)
-    job_stage(3, 2)
+    job_stage(2, 1)
 
     @pl.loop(0, NT // GROUP)
     def _(g):
         put_rows(g2f, g * GROUP, rows_of(g2f, g * GROUP) + dot_nt(rows_of(mbuf, g * GROUP), wm[...]))
 
+    job_stage(0, 4)
     job_stage(1, 3)
-    job_stage(0, 4)
-    last_stage(2)
+    job_stage(2, 2)
     job_stage(2, 3)
-    job_stage(3, 3)
-    job_stage(1, 4)
-    job_stage(0, 5)
-    last_stage(3)
-    job_stage(2, 4)
-    job_stage(3, 4)
-    job_stage(1, 5)
-    job_stage(0, 6)
-    job_stage(2, 5)
-    job_stage(3, 5)
-    job_stage(1, 6)
-    last_stage(4)
-    job_stage(2, 6)
-    job_stage(3, 6)
     for d in range(4):
         when(back_from[d], lambda d=d: back_copy(d).wait_recv())
     for e in range(8):
@@ -671,9 +536,10 @@
 
     lat_out = pltpu.make_async_copy(agg, lat_hbm, out_sem.at[0])
     lat_out.start()
+    job_stage(1, 4)
+    job_stage(2, 4)
     for j in range(len(JOBS)):
-        job_stage(j, 7)
-    last_stage(5)
+        job_stage(j, 5)
     lat_out.wait()
     for d in range(4):
         when(back_has[d], lambda d=d: back_copy(d).wait_send())
@@ -736,18 +602,15 @@
         pltpu.VMEM((TILE, D), F32),
         pltpu.VMEM((GRAD_F32, D), F32),
         pltpu.VMEM((GRAD_ROWS, HALF), BF16), pltpu.VMEM((GRAD_ROWS, HALF), BF16),
-        pltpu.VMEM((n - 1, LAST // n, HALF), BF16), pltpu.VMEM((LAST // n, HALF), BF16),
-        pltpu.VMEM((n - 1, LAST // n**2, HALF), BF16), pltpu.VMEM((n, GRAD_ROWS // n**2, HALF), BF16),
-        pltpu.VMEM((n * n - 1, LAST_ROWS // n**2, HALF), BF16),
+        pltpu.VMEM((n * n - 1, GRAD_ROWS // n**2, HALF), BF16), pltpu.VMEM((n, GRAD_ROWS // n**2, HALF), BF16),
         tiles(8),
         pltpu.VMEM((24, 128), jnp.int32), pltpu.SMEM((24, 128), jnp.int32),
         pltpu.SemaphoreType.DMA((9 + NT,)), pltpu.SemaphoreType.DMA((2,)), pltpu.SemaphoreType.DMA((1,)),
         *[pltpu.SemaphoreType.DMA((4,))] * 2,
         *[pltpu.SemaphoreType.DMA((2,))] * 4,
         *[pltpu.SemaphoreType.DMA((4,))] * 2,
-        *[pltpu.SemaphoreType.DMA((len(JOBS), JOB_SEMS))] * 2,
-        pltpu.SemaphoreType.DMA((len(JOBS) + 1,)),
-        *[pltpu.SemaphoreType.DMA((2 * n * n + n,))] * 2,
+        *[pltpu.SemaphoreType.DMA((len(JOBS), 2 * n * n + n))] * 2,
+        pltpu.SemaphoreType.DMA((len(JOBS),)),
     ]
     lat, grads = pl.pallas_call(
         functools.partial(kernel, sizes),

time: 122 us -> 127 us (1.041)
  Pallas kernels: 121 us -> 126 us
    pallas_call x1, Pallas kernels: 116 us -> 121 us  [on_device(): pl.pallas_call(functools.partial(kernel, sizes), out_shape=(jax.ShapeDtyp...]
where the time goes in v4:
time: 127 us
  Pallas kernels  126 us (99%)
    pallas_call x1, Pallas kernels, on_device(): pl.pallas_call(functools.partial(kernel, sizes), out_shape=(jax.ShapeDtyp...  121 us
    pallas_call x1, Pallas kernels, on_device(): pl.pallas_call(finish, out_shape=(f32(NT, TILE, D), *[f32(D, D)] * 5, f32...  5.02 us

profile of v4, /device:TPU:1, one launch (start us, length us, event | category | flops | bytes accessed | tf_op | source)
XLA Modules:
  0.0 126.5 jit_solution(9298914147613641134)
XLA Ops:
  0.6 120.7 %mesh_step.1 = (bf16[16,128,512]{2,1,0:T(8,128)(2,1)}, bf16[2,2816,256]{2,1,0:T(8,128)(2,1)}) custom-call(s32[1,4,4]{2,1,0:T(4,128)} %send_ref.1, s32[1,4,16]{2,1,0:T(4,128)} %bitcast.14, s32[1,2,4]{2,1,0:T(2,128)} %dsend_ref.1, s32[3,1,16]{2,1,0:T(1,128)} %bitcast.15, s32[1,16]{1,0:T(1,128)} %mask_ref.1, bf16[16,128,512]{2,1,0:T(8,128)(2,1)} %bitcast.9, ...), custom_call_target="tpu_custom_call" | custom-call | tf_op jit(solution)/shard_map/mesh_step/pallas_call | solution.py:615
  121.3 5.0 %finish.1 = (f32[16,128,512]{2,1,0:T(8,128)}, f32[512,512]{1,0:T(8,128)}, f32[512,512]{1,0:T(8,128)}, f32[512,512]{1,0:T(8,128)}, f32[512,512]{1,0:T(8,128)}, /*index=5*/f32[512,512]{1,0:T(8,128)}, f32[227,512]{1,0:T(8,128)}) custom-call(bf16[16,128,512]{2,1,0:T(8,128)(2,1)} %get-tuple-element.16.lat_hbm, bf16[2,2816,256]{2,1,0:T(8,128)(2,1)} %get-tuple-element.17.grads_hbm), custom_call_target="tpu_custom_call" | custom-call | tf_op jit(solution)/shard_map/finish/pallas_call | solution.py:637

commit v5 on v3

--- a/solution.py
+++ b/solution.py
@@ -616,7 +616,11 @@
         put_rows(usl, d * 4, dot_nt(rows_of(mbuf, NT + d * 4), wm[...]).astype(BF16))
         when(back_has[d], lambda d=d: back_copy(d).start())
 
+    job_stage(0, 3)
+    job_stage(1, 2)
     spread(0, outer_edges, ADJ_EDGES, adjw, pool1)
+    job_stage(2, 2)
+    job_stage(3, 2)
 
     @pl.loop(0, NT)
     def _(e):
@@ -625,32 +629,27 @@
     left, right = [(nv, 0, NT), (halo, 0, NT)], [(mbuf, 0), (mbuf, NT)]
     gradient(LAST, left, right)
     last_stage(0)
-    job_stage(0, 3)
-    job_stage(1, 2)
+    job_stage(1, 3)
+    job_stage(0, 4)
     last_stage(1)
-    job_stage(2, 2)
-    job_stage(3, 2)
+    job_stage(2, 3)
+    job_stage(3, 3)
 
     @pl.loop(0, NT // GROUP)
     def _(g):
         put_rows(g2f, g * GROUP, rows_of(g2f, g * GROUP) + dot_nt(rows_of(mbuf, g * GROUP), wm[...]))
 
-    job_stage(1, 3)
-    job_stage(0, 4)
-    last_stage(2)
-    job_stage(2, 3)
-    job_stage(3, 3)
     job_stage(1, 4)
     job_stage(0, 5)
-    last_stage(3)
     job_stage(2, 4)
     job_stage(3, 4)
+    last_stage(2)
     job_stage(1, 5)
-    job_stage(0, 6)
     job_stage(2, 5)
     job_stage(3, 5)
+    job_stage(0, 6)
+    last_stage(3)
     job_stage(1, 6)
-    last_stage(4)
     job_stage(2, 6)
     job_stage(3, 6)
     for d in range(4):
@@ -671,6 +670,7 @@
 
     lat_out = pltpu.make_async_copy(agg, lat_hbm, out_sem.at[0])
     lat_out.start()
+    last_stage(4)
     for j in range(len(JOBS)):
         job_stage(j, 7)
     last_stage(5)

time: 122 us -> 125 us (1.025)
  Pallas kernels: 121 us -> 124 us
    pallas_call x1, Pallas kernels: 116 us -> 119 us  [on_device(): pl.pallas_call(functools.partial(kernel, sizes), out_shape=(jax.ShapeDtyp...]
where the time goes in v5:
time: 125 us; the launch traced here: 124 us
  Pallas kernels  124 us (99%)
    pallas_call x1, Pallas kernels, on_device(): pl.pallas_call(functools.partial(kernel, sizes), out_shape=(jax.ShapeDtyp...  119 us
    pallas_call x1, Pallas kernels, on_device(): pl.pallas_call(finish, out_shape=(f32(NT, TILE, D), *[f32(D, D)] * 5, f32...  5.02 us

profile of v5, /device:TPU:1, one launch (start us, length us, event | category | flops | bytes accessed | tf_op | source)
XLA Modules:
  0.0 124.4 jit_solution(7997244906970634071)
XLA Ops:
  0.6 118.5 %mesh_step.1 = (bf16[16,128,512]{2,1,0:T(8,128)(2,1)}, bf16[2,2816,256]{2,1,0:T(8,128)(2,1)}) custom-call(s32[1,4,4]{2,1,0:T(4,128)} %send_ref.1, s32[1,4,16]{2,1,0:T(4,128)} %bitcast.14, s32[1,2,4]{2,1,0:T(2,128)} %dsend_ref.1, s32[3,1,16]{2,1,0:T(1,128)} %bitcast.15, s32[1,16]{1,0:T(1,128)} %mask_ref.1, bf16[16,128,512]{2,1,0:T(8,128)(2,1)} %bitcast.9, ...), custom_call_target="tpu_custom_call" | custom-call | tf_op jit(solution)/shard_map/mesh_step/pallas_call | solution.py:752
  119.2 5.0 %finish.1 = (f32[16,128,512]{2,1,0:T(8,128)}, f32[512,512]{1,0:T(8,128)}, f32[512,512]{1,0:T(8,128)}, f32[512,512]{1,0:T(8,128)}, f32[512,512]{1,0:T(8,128)}, /*index=5*/f32[512,512]{1,0:T(8,128)}, f32[227,512]{1,0:T(8,128)}) custom-call(bf16[16,128,512]{2,1,0:T(8,128)(2,1)} %get-tuple-element.16.lat_hbm, bf16[2,2816,256]{2,1,0:T(8,128)(2,1)} %get-tuple-element.17.grads_hbm), custom_call_target="tpu_custom_call" | custom-call | tf_op jit(solution)/shard_map/finish/pallas_call | solution.py:774

commit v6 on v3

--- a/solution.py
+++ b/solution.py
@@ -625,34 +625,34 @@
     left, right = [(nv, 0, NT), (halo, 0, NT)], [(mbuf, 0), (mbuf, NT)]
     gradient(LAST, left, right)
     last_stage(0)
-    job_stage(0, 3)
-    job_stage(1, 2)
-    last_stage(1)
     job_stage(2, 2)
     job_stage(3, 2)
+    last_stage(1)
+    job_stage(1, 2)
+    job_stage(0, 3)
 
     @pl.loop(0, NT // GROUP)
     def _(g):
         put_rows(g2f, g * GROUP, rows_of(g2f, g * GROUP) + dot_nt(rows_of(mbuf, g * GROUP), wm[...]))
 
+    job_stage(2, 3)
+    job_stage(3, 3)
+    last_stage(2)
     job_stage(1, 3)
     job_stage(0, 4)
-    last_stage(2)
-    job_stage(2, 3)
-    job_stage(3, 3)
+    job_stage(2, 4)
+    job_stage(3, 4)
+    last_stage(3)
     job_stage(1, 4)
     job_stage(0, 5)
-    last_stage(3)
-    job_stage(2, 4)
-    job_stage(3, 4)
+    job_stage(2, 5)
+    job_stage(3, 5)
     job_stage(1, 5)
     job_stage(0, 6)
-    job_stage(2, 5)
-    job_stage(3, 5)
-    job_stage(1, 6)
     last_stage(4)
     job_stage(2, 6)
     job_stage(3, 6)
+    job_stage(1, 6)
     for d in range(4):
         when(back_from[d], lambda d=d: back_copy(d).wait_recv())
     for e in range(8):

time: 122 us -> 119 us (0.975)
  Pallas kernels: 121 us -> 118 us
    pallas_call x1, Pallas kernels: 116 us -> 113 us  [on_device(): pl.pallas_call(functools.partial(kernel, sizes), out_shape=(jax.ShapeDtyp...]
where the time goes in v6:
time: 119 us
  Pallas kernels  118 us (99%)
    pallas_call x1, Pallas kernels, on_device(): pl.pallas_call(functools.partial(kernel, sizes), out_shape=(jax.ShapeDtyp...  113 us
    pallas_call x1, Pallas kernels, on_device(): pl.pallas_call(finish, out_shape=(f32(NT, TILE, D), *[f32(D, D)] * 5, f32...  5.02 us

profile of v6, /device:TPU:1, one launch (start us, length us, event | category | flops | bytes accessed | tf_op | source)
XLA Modules:
  0.0 119.0 jit_solution(6792498487939597384)
XLA Ops:
  0.6 113.2 %mesh_step.1 = (bf16[16,128,512]{2,1,0:T(8,128)(2,1)}, bf16[2,2816,256]{2,1,0:T(8,128)(2,1)}) custom-call(s32[1,4,4]{2,1,0:T(4,128)} %send_ref.1, s32[1,4,16]{2,1,0:T(4,128)} %bitcast.14, s32[1,2,4]{2,1,0:T(2,128)} %dsend_ref.1, s32[3,1,16]{2,1,0:T(1,128)} %bitcast.15, s32[1,16]{1,0:T(1,128)} %mask_ref.1, bf16[16,128,512]{2,1,0:T(8,128)(2,1)} %bitcast.9, ...), custom_call_target="tpu_custom_call" | custom-call | tf_op jit(solution)/shard_map/mesh_step/pallas_call | solution.py:752
  113.8 5.0 %finish.1 = (f32[16,128,512]{2,1,0:T(8,128)}, f32[512,512]{1,0:T(8,128)}, f32[512,512]{1,0:T(8,128)}, f32[512,512]{1,0:T(8,128)}, f32[512,512]{1,0:T(8,128)}, /*index=5*/f32[512,512]{1,0:T(8,128)}, f32[227,512]{1,0:T(8,128)}) custom-call(bf16[16,128,512]{2,1,0:T(8,128)(2,1)} %get-tuple-element.16.lat_hbm, bf16[2,2816,256]{2,1,0:T(8,128)(2,1)} %get-tuple-element.17.grads_hbm), custom_call_target="tpu_custom_call" | custom-call | tf_op jit(solution)/shard_map/finish/pallas_call | solution.py:774
